TPU v7x, 256 devices: a whole 4x4x8 slice. The times are simulated.
256 devices in a mesh: ctx: 32 (over z, y_lo, core), dec: 8 (over x, y_hi).
Axes of the slice: x: 4, y: 4 (y_hi: 2, y_lo: 2; y = y_hi * 2 + y_lo), z: 8, core: 2. Of those that a mesh axis runs over, the one named last changes fastest.
Arguments:
- hidden: bfloat16 [4096, 7168], P('ctx', 'dec'), may hold values from -6 to 6
- kv_weight: bfloat16 [7168, 576], P('dec'), may hold values from -0.0625 to 0.0625
- kv_gain: float32 [512], replicated, may hold values from 0.1 to 1.9
- queries: bfloat16 [4096, 64, 576], P('ctx', 'dec'), may hold values from -28 to 28
- group_order: int32 [64], replicated, may hold values from 0 to 63, as said below
- page_owner: int32 [32, 32], replicated, may hold values from 0 to 31, as said below
- page_slot: int32 [32, 32], replicated, may hold values from 0 to 31, as said below
Outputs:
- attended: bfloat16 [4096, 64, 512], P('ctx', 'dec')
- paged_cache: bfloat16 [1024, 2304], P('ctx')
Inputs may be any that keep to these rules, and one draw needn't show every extreme that they name: `group_order`: each index of ctx holds two mirror blocks: some block b and the block b places from the end, in either order; every block appears once. `page_owner`: each row names every owner exactly 32 / 32 times. `page_slot`: the pages that reach one owner take its 32 slots once each.
All inputs are finite; a program needn't handle non-finite values.
Results may differ from a plain program's by a relative error of at most 0.012.
Values may be sent and summed in bfloat16 or wider, within the bound.
A program may use at most 128 MiB of HBM per device.

v0:
```python
import jax
import jax.numpy as jnp
from jax import lax
from jax.sharding import PartitionSpec as P

SOFTMAX_SCALE = 192.0 ** (-0.5)
NORM_EPS = 1e-06


def row_positions(row_index, group_order, half_rows):
    block_index = row_index // half_rows
    table = jnp.arange(group_order.shape[0], dtype=jnp.int32)
    picked = jnp.sum(
        jnp.where(block_index[:, None] == table[None, :], group_order[None, :], 0), axis=1
    )
    return picked * half_rows + row_index % half_rows


def finish_rows(projected, kv_gain, positions):
    width = kv_gain.shape[0]
    latent_part = projected[:, :width]
    scaled = (
        latent_part
        * lax.rsqrt(jnp.mean(latent_part * latent_part, axis=1, keepdims=True) + NORM_EPS)
        * kv_gain
    )
    rope_part = projected[:, width:]
    half_width = rope_part.shape[1] // 2
    frequency = 10000.0 ** (-(2.0 * jnp.arange(half_width, dtype=jnp.float32)) / rope_part.shape[1])
    angles = positions.astype(jnp.float32)[:, None] * frequency[None, :]
    first_half = rope_part[:, :half_width]
    second_half = rope_part[:, half_width:]
    cosine = jnp.cos(angles)
    sine = jnp.sin(angles)
    rotated = jnp.concatenate(
        [first_half * cosine - second_half * sine, first_half * sine + second_half * cosine], axis=1
    )
    return jnp.concatenate([scaled, rotated], axis=1).astype(jnp.bfloat16)


def make_fold(queries, query_pos, group_order, half_rows, width):

    def work(state_now, key_piece, key_pos):
        running_max, denominator, accumulated = state_now
        scores = (
            jnp.einsum("rhk,nk->rhn", queries, key_piece, preferred_element_type=jnp.float32)
            * SOFTMAX_SCALE
        )
        allowed = key_pos[None, None, :] <= query_pos[:, None, None]
        new_max = jnp.maximum(running_max, jnp.max(jnp.where(allowed, scores, -1e30), axis=-1))
        weights = jnp.where(allowed, jnp.exp(scores - new_max[..., None]), 0.0)
        denominator = jnp.sum(weights, axis=-1)
        low_weights = weights.astype(jnp.bfloat16)
        mixed = jnp.einsum(
            "rhn,nv->rhv", low_weights, key_piece[:, :width], preferred_element_type=jnp.float32
        )
        accumulated = mixed
        return (new_max, denominator, accumulated)

    def fold(state_now, key_piece, first_row):
        attn_state, page_buffer = state_now
        row_ids = jnp.arange(key_piece.shape[0], dtype=jnp.int32)
        key_pos = row_positions(row_ids, group_order, half_rows)
        attn_state = work(attn_state, key_piece, key_pos)
        return (attn_state, page_buffer)

    return fold


def body(hidden, kv_weight, kv_gain, queries, group_order, page_owner, page_slot):
    tok_rows = hidden.shape[0]
    width = kv_gain.shape[0]
    half_rows = tok_rows // 2
    ctx_index = lax.axis_index("ctx")
    page_count = page_owner.shape[1]
    owner_count = page_owner.shape[0]
    page_rows = tok_rows // page_count
    row_width = kv_weight.shape[1]
    query_pos = row_positions(
        ctx_index * tok_rows + jnp.arange(tok_rows, dtype=jnp.int32), group_order, half_rows
    )
    fold = make_fold(queries, query_pos, group_order, half_rows, width)
    head_count = queries.shape[1]
    attn_start = (
        jnp.full((tok_rows, head_count), -1e30, jnp.float32),
        jnp.zeros((tok_rows, head_count), jnp.float32),
        jnp.zeros((tok_rows, head_count, width), jnp.float32),
    )
    start_state = (attn_start, jnp.zeros((page_count * page_rows, row_width), jnp.bfloat16))
    partial_proj = jnp.dot(hidden, kv_weight, preferred_element_type=jnp.float32)
    summed = lax.psum(partial_proj, "dec")
    block_cache = finish_rows(summed, kv_gain, query_pos)
    final_state = fold(
        start_state, lax.all_gather(block_cache, "ctx", axis=0, tiled=True), jnp.int32(0)
    )
    attn_state, page_buffer = final_state
    attended = (attn_state[2] / attn_state[1][..., None]).astype(jnp.bfloat16)
    per_owner = page_count // owner_count
    page_values = block_cache.reshape(page_count, -1)
    owner_row = lax.dynamic_index_in_dim(page_owner, ctx_index, 0, keepdims=False)
    slot_row = lax.dynamic_index_in_dim(page_slot, ctx_index, 0, keepdims=False)
    sort_order = jnp.argsort(owner_row * page_count + jnp.arange(page_count, dtype=jnp.int32))
    sorted_pages = page_values[sort_order].reshape(owner_count, per_owner, -1)
    sorted_slots = slot_row[sort_order].reshape(owner_count, per_owner)
    received, received_slots = (
        lax.all_to_all(sorted_pages, "ctx", split_axis=0, concat_axis=0, tiled=True),
        lax.all_to_all(sorted_slots, "ctx", split_axis=0, concat_axis=0, tiled=True),
    )
    placing = jnp.argsort(received_slots.reshape(-1))
    paged_cache = received.reshape(page_count, -1)[placing]
    return (attended, paged_cache)


def solution(mesh):
    return jax.shard_map(
        body,
        mesh=mesh,
        in_specs=(P("ctx", "dec"), P("dec", None), P(), P("ctx", "dec", None), P(), P(), P()),
        out_specs=(P("ctx", "dec", None), P("ctx", None)),
        check_vma=False,
    )
```

profile of v0, /device:TPU:1, one launch (start us, length us, event | category | flops | bytes accessed | tf_op | source)
XLA Modules:
  0.0 226.7 jit_solution(3931424910367876107)
XLA Ops:
  7.2 2.6 %fusion.34 = f32[128,576]{0,1:T(8,128)} fusion(bf16[128,896]{1,0:T(8,128)(2,1)} %param.7, bf16[896,576]{0,1:T(8,128)(2,1)} %param.8), kind=kOutput, calls=%fused_computation.67 | convolution fusion | flops 132120576 | bytes 1556480 | tf_op jit(solution)/shard_map/dot_general | solution.py:90
  9.9 0.7 select_reduce_fusion.1
  10.7 88.9 %all-reduce.2.cloned.1.call-done = f32[128,576]{0,1:T(8,128)} async-done(((f32[128,576]{0,1:T(8,128)}), f32[128,576]{0,1:T(8,128)}) %all-reduce.2.cloned.1.call-update) | async-done | bytes 294928 | tf_op jit(solution)/shard_map/psum | solution.py:91
  99.5 1.0 multiply_reduce_fusion
  100.6 0.9 fusion.25
  101.5 1.1 multiply_multiply_fusion
  103.3 0.7 bitcast_add_fusion
  104.0 1.6 sort.31
  107.0 0.7 copy.32
  107.7 13.1 %all-to-all-start.1 = ((s32[32,1,1]{2,1,0:T(1,128)}), s32[32,1,1]{2,1,0:T(1,128)S(1)}, u32[]{:S(2)}, u32[]{:S(2)}) async-start(s32[32,1,1]{2,1,0:T(1,128)} %copy.32), calls=%async_computation.1 | async-start | bytes 32768 | tf_op jit(solution)/shard_map/all_to_all | solution.py:107
  120.8 0.9 select_reduce_fusion
  121.7 1.9 broadcast_compare_fusion
  123.6 5.1 %all-to-all-done.1 = s32[32,1,1]{2,1,0:T(1,128)S(1)} async-done(((s32[32,1,1]{2,1,0:T(1,128)}), s32[32,1,1]{2,1,0:T(1,128)S(1)}, u32[]{:S(2)}, u32[]{:S(2)}) %all-to-all-start.1) | async-done | bytes 160 | tf_op jit(solution)/shard_map/all_to_all | solution.py:107
  129.4 1.6 sort.32
  131.0 1.1 copy.30
  134.1 0.7 reshape.189
  134.8 4.2 %all-to-all-start = ((bf16[32,2,1152]{2,1,0:T(2,128)(2,1)}), bf16[32,2,1152]{2,1,0:T(2,128)(2,1)S(1)}, u32[]{:S(2)}, u32[]{:S(2)}) async-start(bf16[32,2,1152]{2,1,0:T(2,128)(2,1)} %reshape.189), calls=%async_computation | async-start | bytes 294912 | tf_op jit(solution)/shard_map/all_to_all | solution.py:106
  139.0 11.1 %all-to-all-done = bf16[32,2,1152]{2,1,0:T(2,128)(2,1)S(1)} async-done(((bf16[32,2,1152]{2,1,0:T(2,128)(2,1)}), bf16[32,2,1152]{2,1,0:T(2,128)(2,1)S(1)}, u32[]{:S(2)}, u32[]{:S(2)}) %all-to-all-start) | async-done | bytes 147488 | tf_op jit(solution)/shard_map/all_to_all | solution.py:106
  150.2 1.3 gather_fusion.2
  151.5 32.8 %all-gather.2.cloned.1.call-done = bf16[4096,576]{0,1:T(8,128)(2,1)} async-done(((bf16[128,576]{0,1:T(8,128)(2,1)}), bf16[4096,576]{0,1:T(8,128)(2,1)}) %all-gather.2.cloned.1.call-update) | async-done | bytes 4718608 | tf_op jit(solution)/shard_map/all_gather | solution.py:94
  184.3 13.2 %fusion = (f32[128,8]{0,1:T(8,128)S(1)}, f32[4096,128,8]{1,0,2:T(8,128)}) fusion(pred[128,4096]{0,1:T(8,128)(4,1)S(1)} %broadcast_compare_fusion, bf16[128,8,576]{0,2,1:T(8,128)(2,1)S(1)} %copy-done, bf16[4096,576]{0,1:T(8,128)(2,1)} %all-gather.2.cloned.1.call-done), kind=kOutput, calls=%fused_computation.5 | convolution fusion | flops 4844420096 | bytes 23203840 | tf_op jit(solution)/shard_map/rhk,nk->rhn/dot_general | solution.py:46
  197.5 9.2 %fusion.3 = f32[128,8]{0,1:T(8,128)S(1)} fusion(f32[4096,128,8]{1,0,2:T(8,128)} %get-tuple-element.21, f32[128,8]{0,1:T(8,128)S(1)} %broadcast_maximum_fusion, pred[128,4096]{0,1:T(8,128)(4,1)S(1)} %broadcast_compare_fusion), kind=kLoop, calls=%fused_computation.8 | loop fusion | flops 16776192 | bytes 17309696 | tf_op jit(solution)/shard_map/reduce_sum | solution.py:52
  206.7 11.6 %divide_convert_fusion = bf16[128,8,512]{2,0,1:T(8,128)(2,1)S(1)} fusion(f32[128,8]{0,1:T(8,128)S(1)} %fusion.3, bf16[4096,576]{0,1:T(8,128)(2,1)} %all-gather.2.cloned.1.call-done, f32[4096,128,8]{1,0,2:T(8,128)} %get-tuple-element.21, f32[128,8]{0,1:T(8,128)S(1)} %broadcast_maximum_fusion, pred[128,4096]{0,1:T(8,128)(4,1)S(1)} %broadcast_compare_fusion), kind=kOutput, calls=%fused_computation.18 | convolution fusion | flops 4312793088 | bytes 22552576 | tf_op jit(solution)/shard_map/rhn,nv->rhv/dot_general | solution.py:54
  218.3 1.5 copy.33
  (29 shorter events, 5.1 us)
Async XLA Ops:
  7.2 177.2 %copy-start = (bf16[128,8,576]{0,2,1:T(8,128)(2,1)S(1)}, bf16[128,8,576]{0,2,1:T(8,128)(2,1)}, u32[]{:S(2)}) copy-start(bf16[128,8,576]{0,2,1:T(8,128)(2,1)} %param.10) | copy-start | bytes 3538948
  7.2 92.4 %all-reduce.2.cloned.1.call-start = ((), (), s32[]{:S(2)}) async-start(), calls=%async_computation.2 | async-start | bytes 589824 | tf_op jit(solution)/shard_map/psum | solution.py:91
  9.8 174.5 %all-gather.2.cloned.1.call-start = ((), (), s32[]{:S(2)}) async-start(), calls=%async_computation.3 | async-start | bytes 4866048 | tf_op jit(solution)/shard_map/all_gather | solution.py:94
  107.7 21.0 %all-to-all-start.1 = ((s32[32,1,1]{2,1,0:T(1,128)}), s32[32,1,1]{2,1,0:T(1,128)S(1)}, u32[]{:S(2)}, u32[]{:S(2)}) async-start(s32[32,1,1]{2,1,0:T(1,128)} %copy.32), calls=%async_computation.1 | async-start | bytes 32768 | tf_op jit(solution)/shard_map/all_to_all | solution.py:107
  134.8 15.2 %all-to-all-start = ((bf16[32,2,1152]{2,1,0:T(2,128)(2,1)}), bf16[32,2,1152]{2,1,0:T(2,128)(2,1)S(1)}, u32[]{:S(2)}, u32[]{:S(2)}) async-start(bf16[32,2,1152]{2,1,0:T(2,128)(2,1)} %reshape.189), calls=%async_computation | async-start | bytes 294912 | tf_op jit(solution)/shard_map/all_to_all | solution.py:106
Sparse Core Ops, SparseCore 0:
  11.2 88.2 all-reduce.1
  103.4 80.9 all-gather.1
where the time goes:
time: 227 us
  waiting for transfers between devices  138 us (61%)
  matrix products  27.4 us (12%)
  other arithmetic  21.7 us (10%)
  starting transfers between devices  17.4 us (8%)
  between operations  14.2 us (6%)
  local copies, waits for them, and re-layouts  8.22 us (4%)
    psum x1, waiting for transfers between devices, body(): summed = lax.psum(partial_proj, 'dec')  88.9 us
    all_gather x1, waiting for transfers between devices, body(): lax.all_gather(block_cache, 'ctx', axis=0, tiled=True)  32.8 us
    dot_general x1, matrix products, work(): jnp.einsum('rhk,nk->rhn', queries, key_piece, preferred_element_type=jnp....  13.2 us
    all_to_all x1, starting transfers between devices, body(): lax.all_to_all(sorted_slots, 'ctx', split_axis=0, concat_axis=0, tiled=True)  13.1 us
    dot_general x1, matrix products, work(): jnp.einsum('rhn,nv->rhv', low_weights, key_piece[:, :width], preferred_el...  11.6 us
    all_to_all x1, waiting for transfers between devices, body(): lax.all_to_all(sorted_pages, 'ctx', split_axis=0, concat_axis=0, tiled=True)  11.1 us
    reduce_sum x1, other arithmetic, work(): denominator = jnp.sum(weights, axis=-1)  9.16 us
    all_to_all x1, waiting for transfers between devices, body(): lax.all_to_all(sorted_slots, 'ctx', split_axis=0, concat_axis=0, tiled=True)  5.07 us
  transfers between devices with their start and end apart: 4, of which 4 were waited for; matrix products, arithmetic and copies ran while one was open for 7% of the time, Pallas kernels for 0%

commit v1 on v0

v1 whole, which is shorter than its diff:
```python
import functools

import jax
import jax.numpy as jnp
import numpy as np
from jax import lax
from jax.experimental import pallas as pl
from jax.experimental.pallas import tpu as pltpu
from jax.sharding import PartitionSpec as P

MESH = pl.DeviceIdType.MESH
NX, NY, NZ = 4, 4, 8
HALF = 64
ROWS = 128
PIECE = 16
LAT = 512
ROT = 64
HEADS = 8
BLOCK = ROWS + PIECE
CHUNK = 4 * ROWS
PAGES = 32
EPS = 1e-6
LOG2E_SCALE = float(192.0 ** (-0.5) * np.log2(np.e))
NEG = -1e30
TILE_HEADS = 2


def device(x, y, z, core):
    return ((z * 2 + y % 2) * 2 + core, x * 2 + y // 2)


def remote(src, dst, send_sem, recv_sem, target):
    return pltpu.make_async_remote_copy(
        src_ref=src, dst_ref=dst, send_sem=send_sem, recv_sem=recv_sem, device_id=target, device_id_type=MESH
    )


def kernel(
    hidden_hbm, weight_hbm, gain_ref, freq_ref, queries_hbm, order_ref, owner_ref, slot_ref,
    out_ref, paged_ref,
    hid, wt, qt, part, sums, zbuf, gath, ql, qr, acc, top, den, bias, kpos, drow, page_lat, page_rot, krot,
    in_sem, rs_send, rs_recv, z_send, z_recv, b_send, b_recv, a_send, a_recv, s_send, s_recv,
):
    ctx = lax.axis_index("ctx")
    dec = lax.axis_index("dec")
    core = ctx % 2
    z = ctx // 4
    x = dec // 2
    y = (dec % 2) * 2 + (ctx // 2) % 2
    first = core == 0
    a = jnp.where(first, x, y)
    b = jnp.where(first, y, x)

    def at_ab(aa, bb):
        return device(jnp.where(first, aa, bb), jnp.where(first, bb, aa), z, core)

    rs_offsets = [(dx, dy) for dx in range(NX) for dy in range(2)][1:]

    def rs_device(dx, dy, sign):
        xx = (x + sign * dx + NX) % NX
        yh = (dec % 2 + dy) % 2
        return ctx, xx * 2 + yh

    barrier = pltpu.get_barrier_semaphore()
    partners = [rs_device(dx, dy, 1) for dx, dy in rs_offsets]
    partners += [device(x, y, (z + dz) % NZ, core) for dz in range(1, NZ)]
    partners += [at_ab(a, (b + d) % 4) for d in range(1, 4)]
    partners += [at_ab((a + d) % 4, b) for d in range(1, 4)]
    partners += [device(x, y, z, 1 - core)]
    for target in partners:
        pl.semaphore_signal(barrier, inc=1, device_id=target, device_id_type=MESH)

    loads = [
        pltpu.make_async_copy(hidden_hbm, hid, in_sem.at[0]),
        pltpu.make_async_copy(weight_hbm, wt, in_sem.at[1]),
        pltpu.make_async_copy(queries_hbm, qt, in_sem.at[2]),
    ]
    for load in loads:
        load.start()
    loads[0].wait()
    loads[1].wait()
    part[...] = lax.dot_general(
        hid[...], wt[...], (((1,), (1,)), ((), ())), preferred_element_type=jnp.float32
    ).reshape(part.shape)
    pl.semaphore_wait(barrier, len(partners))

    scatter = []
    for k, (dx, dy) in enumerate(rs_offsets):
        target = rs_device(dx, dy, 1)
        scatter.append(remote(part.at[target[1]], sums.at[k], rs_send.at[k], rs_recv.at[k], target))
        scatter[-1].start()

    start_pos = order_ref[ctx * 2 + dec // 4] * HALF + (dec % 4) * PIECE
    my_pos = (start_pos + lax.broadcasted_iota(jnp.int32, (PIECE, 128), 0)).astype(jnp.float32)
    angle = my_pos * freq_ref[...]
    cosine = jnp.cos(angle)
    sine = jnp.sin(angle)

    lane = lax.broadcasted_iota(jnp.int32, (1, ROWS), 1)
    lane_z = lane // PIECE
    lane_i = lane % PIECE
    mine = owner_ref[...] == ctx
    page_id = lax.broadcasted_iota(jnp.int32, (PAGES, PAGES), 1).astype(jnp.float32)
    page_of = jnp.sum(jnp.where(mine, page_id, 0.0), axis=1, keepdims=True)
    slot_of = jnp.sum(jnp.where(mine, slot_ref[...].astype(jnp.float32), 0.0), axis=1, keepdims=True)
    ctx_id = lax.broadcasted_iota(jnp.int32, (PAGES, ROWS), 0)
    ctx_lane = lax.broadcasted_iota(jnp.int32, (PAGES, ROWS), 1) // PIECE
    for cc in range(2):
        for ylo in range(2):
            picks = ctx_id == ctx_lane * 4 + (ylo * 2 + cc)
            page_z = jnp.sum(jnp.where(picks, page_of, 0.0), axis=0, keepdims=True).astype(jnp.int32)
            slot_z = jnp.sum(jnp.where(picks, slot_of, 0.0), axis=0, keepdims=True).astype(jnp.int32)
            for xhi in range(2):
                base = jnp.zeros((1, ROWS), jnp.int32)
                for zz in range(NZ):
                    base = jnp.where(lane_z == zz, order_ref[((zz * 2 + ylo) * 2 + cc) * 2 + xhi] * HALF, base)
                for xlo in range(2):
                    for yhi in range(2):
                        xx, yy = xhi * 2 + xlo, yhi * 2 + ylo
                        aa, bb = (xx, yy) if cc == 0 else (yy, xx)
                        row, cols = cc * 4 + aa, slice(bb * ROWS, (bb + 1) * ROWS)
                        kpos[row : row + 1, cols] = base + (xlo * 2 + yhi) * PIECE + lane_i
                        page = (xx * 2 + yhi) * 4 + lane_i // 4
                        drow[row : row + 1, cols] = jnp.where(page_z == page, (lane_i % 4) * PAGES + slot_z, -1)

    loads[2].wait()
    for h in range(HEADS):
        ql[h * ROWS : (h + 1) * ROWS, :] = qt[h, :LAT, :].T
        turned = qt[h, LAT:, :].T
        qr[h * ROWS : (h + 1) * ROWS, :] = jnp.concatenate([turned, turned], axis=1)
    acc[...] = jnp.zeros_like(acc)
    den[...] = jnp.zeros_like(den)
    top[...] = jnp.full_like(top, NEG)
    page_lat[...] = jnp.zeros_like(page_lat)
    page_rot[...] = jnp.zeros_like(page_rot)

    total = part[dec]
    for k, copy in enumerate(scatter):
        copy.wait_recv()
        total = total + sums[k]

    latent = total[:, :LAT]
    inverse = lax.rsqrt(jnp.mean(latent * latent, axis=1, keepdims=True) + EPS)
    latent = latent * inverse * gain_ref[...]
    half = ROT // 2
    r1, r2 = total[:, LAT : LAT + half], total[:, LAT + half :]
    c1, s1 = cosine[:, :half], sine[:, :half]
    turned = jnp.concatenate([r1 * c1 - r2 * s1, r1 * s1 + r2 * c1], axis=1)
    zbuf[z] = jnp.concatenate([latent, turned, turned], axis=1).astype(jnp.bfloat16)

    along_z = []
    for dz in range(1, NZ):
        copy = remote(zbuf.at[z], zbuf.at[z], z_send.at[dz], z_recv.at[dz], device(x, y, (z + dz) % NZ, core))
        copy.start()
        along_z.append(copy)
    for dz in range(1, NZ):
        came = (z - dz + NZ) % NZ
        remote(
            zbuf.at[came], zbuf.at[came], z_send.at[dz], z_recv.at[dz], device(x, y, (z + dz) % NZ, core)
        ).wait_recv()
    left = lax.broadcasted_iota(jnp.int32, (PIECE, 128), 1) < ROT
    mine_block = gath.at[core, a, b]
    for zz in range(NZ):
        mine_block[zz * PIECE : (zz + 1) * PIECE, :] = zbuf[zz, :, :LAT]
    for pair in range(NZ // 2):
        mine_block[ROWS:, pair * 128 : (pair + 1) * 128] = jnp.where(
            left, zbuf[2 * pair, :, LAT:], zbuf[2 * pair + 1, :, LAT:]
        )

    along_b = []
    for d in range(1, 4):
        copy = remote(mine_block, mine_block, b_send.at[d], b_recv.at[d], at_ab(a, (b + d) % 4))
        copy.start()
        along_b.append(copy)
    for d in range(1, 4):
        came = gath.at[core, a, (b - d + 4) % 4]
        remote(came, came, b_send.at[d], b_recv.at[d], at_ab(a, (b + d) % 4)).wait_recv()

    along_a = []
    strip = gath.at[core, a]
    for d in (1, 3, 2):
        copy = remote(strip, strip, a_send.at[d], a_recv.at[d], at_ab((a + d) % 4, b))
        copy.start()
        along_a.append(copy)

    token = lax.broadcasted_iota(jnp.int32, (ROWS, CHUNK), 0)
    q_pos = jnp.where(token < HALF, order_ref[ctx * 2], order_ref[ctx * 2 + 1]) * HALF + token % HALF
    page_row = lax.broadcasted_iota(jnp.int32, (ROWS, CHUNK), 0)
    tile_rows = TILE_HEADS * ROWS

    def attend(cc, aa):
        which = cc * 4 + aa
        bias[...] = jnp.where(kpos[pl.ds(which, 1), :] <= q_pos, 0.0, NEG)
        pick = jnp.where(drow[pl.ds(which, 1), :] == page_row, 1.0, 0.0).astype(jnp.bfloat16)
        for bb in range(4):
            for zz in range(NZ):
                rot = gath[cc, aa, bb, ROWS:, (zz // 2) * 128 : (zz // 2 + 1) * 128]
                keep = left if zz % 2 == 0 else jnp.logical_not(left)
                krot[bb * ROWS + zz * PIECE : bb * ROWS + (zz + 1) * PIECE, :] = jnp.where(
                    keep, rot, jnp.zeros_like(rot)
                )

        def keys():
            return jnp.concatenate([gath[cc, aa, bb, :ROWS, :] for bb in range(4)], axis=0)

        page_lat[...] += jnp.dot(pick, keys(), preferred_element_type=jnp.float32)
        page_rot[...] += jnp.dot(pick, krot[...], preferred_element_type=jnp.float32)

        @pl.loop(0, HEADS // TILE_HEADS)
        def _(tile):
            rows = pl.ds(pl.multiple_of(tile * tile_rows, tile_rows), tile_rows)
            nt = (((1,), (1,)), ((), ()))
            scores = lax.dot_general(ql[rows, :], keys(), nt, preferred_element_type=jnp.float32)
            scores += lax.dot_general(qr[rows, :], krot[...], nt, preferred_element_type=jnp.float32)
            scores += jnp.concatenate([bias[...]] * TILE_HEADS, axis=0)
            old = top[rows, :]
            new = jnp.maximum(old, jnp.max(scores, axis=1, keepdims=True))
            alpha = jnp.exp2((old - new) * LOG2E_SCALE)
            weights = jnp.exp2((scores - jnp.concatenate([new] * 4, axis=1)) * LOG2E_SCALE)
            top[rows, :] = new
            den[rows, :] = den[rows, :] * alpha + (
                (weights[:, :128] + weights[:, 128:256]) + (weights[:, 256:384] + weights[:, 384:])
            )
            mixed = jnp.dot(weights.astype(jnp.bfloat16), keys(), preferred_element_type=jnp.float32)
            acc[rows, :] = acc[rows, :] * jnp.concatenate([alpha] * 4, axis=1) + mixed

    sibling = device(x, y, z, 1 - core)

    @pl.loop(0, 4)
    def _(k):
        d = k ^ (k // 2)
        aa = (a - d + 4) % 4
        here = gath.at[core, aa]

        @pl.when(k > 0)
        def _():
            remote(here, here, a_send.at[d], a_recv.at[d], at_ab((a + d) % 4, b)).wait_recv()

        remote(here, here, s_send.at[d], s_recv.at[d], sibling).start()
        attend(core, aa)
        theirs = (b - d + 4) % 4
        there = gath.at[1 - core, theirs]
        remote(there, there, s_send.at[d], s_recv.at[d], sibling).wait_recv()
        attend(1 - core, theirs)

    @pl.loop(0, HEADS)
    def _(h):
        rows = pl.ds(pl.multiple_of(h * ROWS, ROWS), ROWS)
        whole = jnp.sum(den[rows, :], axis=1, keepdims=True)
        out_ref[h] = (acc[rows, :] / whole).astype(jnp.bfloat16)

    rotated = page_rot[:, :ROT] + page_rot[:, ROT:]
    width = LAT + ROT
    for j in range(4):
        rows = slice(j * PAGES, (j + 1) * PAGES)
        paged_ref[:, j * width : j * width + LAT] = page_lat[rows, :].astype(jnp.bfloat16)
        paged_ref[:, j * width + LAT : (j + 1) * width] = rotated[rows, :].astype(jnp.bfloat16)

    for copy in scatter + along_z + along_b + along_a:
        copy.wait_send()
    for d in range(4):
        here = gath.at[core, (a - d + 4) % 4]
        remote(here, here, s_send.at[d], s_recv.at[d], sibling).wait_send()


def body(hidden, kv_weight, kv_gain, queries, group_order, page_owner, page_slot):
    half = ROT // 2
    freq = 10000.0 ** (-(2.0 * np.arange(half, dtype=np.float32)) / ROT)
    freq = np.tile(freq.astype(np.float32), 4)[None, :]
    bf, f32 = jnp.bfloat16, jnp.float32
    vmem = pl.BlockSpec(memory_space=pltpu.VMEM)
    hbm = pl.BlockSpec(memory_space=pl.ANY)
    smem = pl.BlockSpec(memory_space=pltpu.SMEM)
    rows = HEADS * ROWS
    dma = pltpu.SemaphoreType.DMA
    attended, paged = pl.pallas_call(
        kernel,
        out_shape=(
            jax.ShapeDtypeStruct((HEADS, ROWS, LAT), bf),
            jax.ShapeDtypeStruct((PAGES, 4 * (LAT + ROT)), bf),
        ),
        in_specs=[hbm, hbm, vmem, vmem, hbm, smem, vmem, vmem],
        out_specs=(vmem, vmem),
        scratch_shapes=[
            pltpu.VMEM(hidden.shape, bf),
            pltpu.VMEM(kv_weight.shape[::-1], bf),
            pltpu.VMEM((HEADS, LAT + ROT, ROWS), bf),
            pltpu.VMEM((8, PIECE, LAT + ROT), f32),
            pltpu.VMEM((7, PIECE, LAT + ROT), f32),
            pltpu.VMEM((NZ, PIECE, LAT + 128), bf),
            pltpu.VMEM((2, 4, 4, BLOCK, LAT), bf),
            pltpu.VMEM((rows, LAT), bf),
            pltpu.VMEM((rows, 128), bf),
            pltpu.VMEM((rows, LAT), f32),
            pltpu.VMEM((rows, 128), f32),
            pltpu.VMEM((rows, 128), f32),
            pltpu.VMEM((ROWS, CHUNK), f32),
            pltpu.VMEM((8, CHUNK), jnp.int32),
            pltpu.VMEM((8, CHUNK), jnp.int32),
            pltpu.VMEM((ROWS, LAT), f32),
            pltpu.VMEM((ROWS, 128), f32),
            pltpu.VMEM((CHUNK, 128), bf),
            dma((3,)), dma((7,)), dma((7,)), dma((8,)), dma((8,)), dma((4,)), dma((4,)), dma((4,)), dma((4,)),
            dma((4,)), dma((4,)),
        ],
        name="cache_attention",
        compiler_params=pltpu.CompilerParams(
            collective_id=0, has_side_effects=True, vmem_limit_bytes=56 * 2**20
        ),
        cost_estimate=pl.CostEstimate(flops=9_000_000_000, bytes_accessed=4_000_000, transcendentals=4_000_000),
    )(
        hidden, kv_weight.T, kv_gain.reshape(1, -1), jnp.asarray(freq), queries.transpose(1, 2, 0),
        group_order, page_owner, page_slot,
    )
    return attended.transpose(1, 0, 2), paged


def solution(mesh):
    return jax.shard_map(
        body,
        mesh=mesh,
        in_specs=(P("ctx", "dec"), P("dec", None), P(), P("ctx", "dec", None), P(), P(), P()),
        out_specs=(P("ctx", "dec", None), P("ctx", None)),
        check_vma=False,
    )
```

time: 227 us -> 73.9 us (0.33)
  waiting for transfers between devices: 138 us -> 0 us
  Pallas kernels: 0 us -> 69.5 us
  matrix products: 27.4 us -> 0 us
  other arithmetic: 21.7 us -> 0 us
  starting transfers between devices: 17.4 us -> 0 us
  between operations: 14.2 us -> 0.65 us
  local copies, waits for them, and re-layouts: 8.22 us -> 3.47 us
    psum x1 -> x0, waiting for transfers between devices: 88.9 us -> none  [body(): summed = lax.psum(partial_proj, 'dec')]
    pallas_call x0 -> x1, Pallas kernels: none -> 69.5 us  [body(): pl.pallas_call(kernel, out_shape=(jax.ShapeDtypeStruct((HEADS, ROWS, LAT)...]
    all_gather x1 -> x0, waiting for transfers between devices: 32.8 us -> none  [body(): lax.all_gather(block_cache, 'ctx', axis=0, tiled=True)]
    dot_general x3 -> x0, matrix products: 27.4 us -> none  [the longest x1 13.2 us: work(): jnp.einsum('rhk,nk->rhn', queries, key_piece, preferred_element_type=jnp....]
    all_to_all x2 -> x0, starting transfers between devices: 17.3 us -> none  [the longest x1 13.1 us: body(): lax.all_to_all(sorted_slots, 'ctx', split_axis=0, concat_axis=0, tiled=True)]
    all_to_all x2 -> x0, waiting for transfers between devices: 16.1 us -> none  [the longest x1 11.1 us: body(): lax.all_to_all(sorted_pages, 'ctx', split_axis=0, concat_axis=0, tiled=True)]
    reduce_sum x4 -> x0, other arithmetic: 11.8 us -> none  [the longest x1 9.16 us: work(): denominator = jnp.sum(weights, axis=-1)]
    sort x2 -> x0, other arithmetic: 3.22 us -> none  [the longest x1 1.61 us: body(): placing = jnp.argsort(received_slots.reshape(-1))]
  transfers between devices with their start and end apart: 4 -> 0, of which waited for: 4 -> 0; matrix products, arithmetic and copies ran while one was open for 7% -> 0% of each run, Pallas kernels for 0% -> 0%
where the time goes in v1:
time: 73.9 us; the launch traced here: 73.7 us
  Pallas kernels  69.5 us (94%)
  local copies, waits for them, and re-layouts  3.47 us (5%)
    pallas_call x1, Pallas kernels, body(): pl.pallas_call(kernel, out_shape=(jax.ShapeDtypeStruct((HEADS, ROWS, LAT)...  69.5 us
    unnamed x4, local copies, waits for them, and re-layouts  3.47 us

profile of v1, /device:TPU:1, one launch (start us, length us, event | category | flops | bytes accessed | tf_op | source)
XLA Modules:
  0.0 73.7 jit_solution(2332971646589201656)
XLA Ops:
  0.6 69.5 %cache_attention.1 = (bf16[8,128,512]{2,1,0:T(8,128)(2,1)}, bf16[32,2304]{1,0:T(8,128)(2,1)}) custom-call(bf16[128,896]{1,0:T(8,128)(2,1)} %hidden_hbm.1, bf16[576,896]{1,0:T(8,128)(2,1)} %bitcast.6, f32[1,512]{1,0:T(1,128)} %bitcast.7, f32[1,128]{1,0:T(1,128)} %constant.2.clone.freq_ref, bf16[8,576,128]{2,1,0:T(8,128)(2,1)} %bitcast.5, s32[64]{0:T(128)} %order_ref.1, ...), custom_call_target="tpu_custom_call" | custom-call | flops 8999999488 | bytes 4000000 | tf_op jit(solution)/shard_map/cache_attention/pallas_call | solution.py:276
  70.2 0.0 copy-start
  70.2 2.8 %copy.10 = bf16[128,8,512]{2,1,0:T(8,128)(2,1)} copy(bf16[128,8,512]{2,0,1:T(8,128)(2,1)} %bitcast.4) | data formatting | bytes 2097152
  73.0 0.0 copy-done
  73.0 0.7 copy.12
Async XLA Ops:
  70.2 2.8 %copy-start = (bf16[32,2304]{1,0:T(8,128)(2,1)S(1)}, bf16[32,2304]{1,0:T(8,128)(2,1)}, u32[]{:S(2)}) copy-start(bf16[32,2304]{1,0:T(8,128)(2,1)} %get-tuple-element.11) | copy-start | bytes 442372

commit v2 on v1

--- a/solution.py
+++ b/solution.py
@@ -22,7 +22,6 @@
 EPS = 1e-6
 LOG2E_SCALE = float(192.0 ** (-0.5) * np.log2(np.e))
 NEG = -1e30
-TILE_HEADS = 2
 
 
 def device(x, y, z, core):
@@ -38,7 +37,7 @@
 def kernel(
     hidden_hbm, weight_hbm, gain_ref, freq_ref, queries_hbm, order_ref, owner_ref, slot_ref,
     out_ref, paged_ref,
-    hid, wt, qt, part, sums, zbuf, gath, ql, qr, acc, top, den, bias, kpos, drow, page_lat, page_rot, krot,
+    hid, wt, qt, part, sums, zbuf, gath, q32, ql, qr, acc, top, den, qpos, kpos, drow, page_lat, page_rot, krot,
     in_sem, rs_send, rs_recv, z_send, z_recv, b_send, b_recv, a_send, a_recv, s_send, s_recv,
 ):
     ctx = lax.axis_index("ctx")
@@ -61,6 +60,14 @@
         yh = (dec % 2 + dy) % 2
         return ctx, xx * 2 + yh
 
+    loads = [
+        pltpu.make_async_copy(hidden_hbm, hid, in_sem.at[0]),
+        pltpu.make_async_copy(weight_hbm, wt, in_sem.at[1]),
+        pltpu.make_async_copy(queries_hbm, qt, in_sem.at[2]),
+    ]
+    for load in loads:
+        load.start()
+
     barrier = pltpu.get_barrier_semaphore()
     partners = [rs_device(dx, dy, 1) for dx, dy in rs_offsets]
     partners += [device(x, y, (z + dz) % NZ, core) for dz in range(1, NZ)]
@@ -70,13 +77,6 @@
     for target in partners:
         pl.semaphore_signal(barrier, inc=1, device_id=target, device_id_type=MESH)
 
-    loads = [
-        pltpu.make_async_copy(hidden_hbm, hid, in_sem.at[0]),
-        pltpu.make_async_copy(weight_hbm, wt, in_sem.at[1]),
-        pltpu.make_async_copy(queries_hbm, qt, in_sem.at[2]),
-    ]
-    for load in loads:
-        load.start()
     loads[0].wait()
     loads[1].wait()
     part[...] = lax.dot_general(
@@ -125,9 +125,15 @@
 
     loads[2].wait()
     for h in range(HEADS):
-        ql[h * ROWS : (h + 1) * ROWS, :] = qt[h, :LAT, :].T
-        turned = qt[h, LAT:, :].T
-        qr[h * ROWS : (h + 1) * ROWS, :] = jnp.concatenate([turned, turned], axis=1)
+        turned = qt[h].T.astype(jnp.float32)
+        turned = jnp.concatenate([turned, turned[:, LAT:]], axis=1)
+        for g in range(5):
+            q32[g, pl.ds(h, ROWS, stride=HEADS), :] = turned[:, g * 128 : (g + 1) * 128]
+    for g in range(4):
+        ql[:, g * 128 : (g + 1) * 128] = q32[g].astype(jnp.bfloat16)
+    qr[...] = q32[4].astype(jnp.bfloat16)
+    token = lax.broadcasted_iota(jnp.int32, qpos.shape, 0) // HEADS
+    qpos[...] = jnp.where(token < HALF, order_ref[ctx * 2], order_ref[ctx * 2 + 1]) * HALF + token % HALF
     acc[...] = jnp.zeros_like(acc)
     den[...] = jnp.zeros_like(den)
     top[...] = jnp.full_like(top, NEG)
@@ -167,30 +173,34 @@
             left, zbuf[2 * pair, :, LAT:], zbuf[2 * pair + 1, :, LAT:]
         )
 
-    along_b = []
-    for d in range(1, 4):
-        copy = remote(mine_block, mine_block, b_send.at[d], b_recv.at[d], at_ab(a, (b + d) % 4))
-        copy.start()
-        along_b.append(copy)
-    for d in range(1, 4):
-        came = gath.at[core, a, (b - d + 4) % 4]
-        remote(came, came, b_send.at[d], b_recv.at[d], at_ab(a, (b + d) % 4)).wait_recv()
-
-    along_a = []
-    strip = gath.at[core, a]
-    for d in (1, 3, 2):
-        copy = remote(strip, strip, a_send.at[d], a_recv.at[d], at_ab((a + d) % 4, b))
-        copy.start()
-        along_a.append(copy)
-
-    token = lax.broadcasted_iota(jnp.int32, (ROWS, CHUNK), 0)
-    q_pos = jnp.where(token < HALF, order_ref[ctx * 2], order_ref[ctx * 2 + 1]) * HALF + token % HALF
+    sibling = device(x, y, z, 1 - core)
+
+    def block(d, e):
+        return gath.at[core, (a - d + 4) % 4, (b - e + 4) % 4]
+
+    def along_b(e):
+        return remote(mine_block, mine_block, b_send.at[e], b_recv.at[e], at_ab(a, (b + e) % 4))
+
+    def along_a(d, e):
+        return remote(block(0, e), block(0, e), a_send.at[d, e], a_recv.at[d, e], at_ab((a + d) % 4, b))
+
+    def across(d, e):
+        return remote(block(d, e), block(d, e), s_send.at[d, e], s_recv.at[d, e], sibling)
+
+    for e in (1, 3, 2):
+        along_b(e).start()
+    for e in (0, 1, 3, 2):
+        if e > 0:
+            came = block(0, e)
+            remote(came, came, b_send.at[e], b_recv.at[e], at_ab(a, (b + e) % 4)).wait_recv()
+        for d in (1, 3, 2):
+            along_a(d, e).start()
+        across(0, e).start()
+
     page_row = lax.broadcasted_iota(jnp.int32, (ROWS, CHUNK), 0)
-    tile_rows = TILE_HEADS * ROWS
 
     def attend(cc, aa):
         which = cc * 4 + aa
-        bias[...] = jnp.where(kpos[pl.ds(which, 1), :] <= q_pos, 0.0, NEG)
         pick = jnp.where(drow[pl.ds(which, 1), :] == page_row, 1.0, 0.0).astype(jnp.bfloat16)
         for bb in range(4):
             for zz in range(NZ):
@@ -206,48 +216,41 @@
         page_lat[...] += jnp.dot(pick, keys(), preferred_element_type=jnp.float32)
         page_rot[...] += jnp.dot(pick, krot[...], preferred_element_type=jnp.float32)
 
-        @pl.loop(0, HEADS // TILE_HEADS)
-        def _(tile):
-            rows = pl.ds(pl.multiple_of(tile * tile_rows, tile_rows), tile_rows)
-            nt = (((1,), (1,)), ((), ()))
-            scores = lax.dot_general(ql[rows, :], keys(), nt, preferred_element_type=jnp.float32)
-            scores += lax.dot_general(qr[rows, :], krot[...], nt, preferred_element_type=jnp.float32)
-            scores += jnp.concatenate([bias[...]] * TILE_HEADS, axis=0)
-            old = top[rows, :]
-            new = jnp.maximum(old, jnp.max(scores, axis=1, keepdims=True))
-            alpha = jnp.exp2((old - new) * LOG2E_SCALE)
-            weights = jnp.exp2((scores - jnp.concatenate([new] * 4, axis=1)) * LOG2E_SCALE)
-            top[rows, :] = new
-            den[rows, :] = den[rows, :] * alpha + (
-                (weights[:, :128] + weights[:, 128:256]) + (weights[:, 256:384] + weights[:, 384:])
-            )
-            mixed = jnp.dot(weights.astype(jnp.bfloat16), keys(), preferred_element_type=jnp.float32)
-            acc[rows, :] = acc[rows, :] * jnp.concatenate([alpha] * 4, axis=1) + mixed
-
-    sibling = device(x, y, z, 1 - core)
+        nt = (((1,), (1,)), ((), ()))
+        scores = lax.dot_general(ql[...], keys(), nt, preferred_element_type=jnp.float32)
+        scores += lax.dot_general(qr[...], krot[...], nt, preferred_element_type=jnp.float32)
+        limit = jnp.concatenate([qpos[...]] * 4, axis=1)
+        scores = jnp.where(kpos[pl.ds(which, 1), :] <= limit, scores, NEG)
+        old = top[...]
+        new = jnp.maximum(old, jnp.max(scores, axis=1, keepdims=True))
+        alpha = jnp.exp2((old - new) * LOG2E_SCALE)
+        weights = jnp.exp2((scores - jnp.concatenate([new] * 4, axis=1)) * LOG2E_SCALE)
+        top[...] = new
+        den[...] = den[...] * alpha + (
+            (weights[:, :128] + weights[:, 128:256]) + (weights[:, 256:384] + weights[:, 384:])
+        )
+        mixed = jnp.dot(weights.astype(jnp.bfloat16), keys(), preferred_element_type=jnp.float32)
+        acc[...] = acc[...] * jnp.concatenate([alpha] * 4, axis=1) + mixed
 
     @pl.loop(0, 4)
     def _(k):
         d = k ^ (k // 2)
-        aa = (a - d + 4) % 4
-        here = gath.at[core, aa]
 
         @pl.when(k > 0)
         def _():
-            remote(here, here, a_send.at[d], a_recv.at[d], at_ab((a + d) % 4, b)).wait_recv()
-
-        remote(here, here, s_send.at[d], s_recv.at[d], sibling).start()
-        attend(core, aa)
+            for e in (0, 1, 3, 2):
+                came = block(d, e)
+                remote(came, came, a_send.at[d, e], a_recv.at[d, e], at_ab((a + d) % 4, b)).wait_recv()
+                across(d, e).start()
+
+        attend(core, (a - d + 4) % 4)
         theirs = (b - d + 4) % 4
-        there = gath.at[1 - core, theirs]
-        remote(there, there, s_send.at[d], s_recv.at[d], sibling).wait_recv()
+        for e in (0, 1, 3, 2):
+            there = gath.at[1 - core, theirs, (a - e + 4) % 4]
+            remote(there, there, s_send.at[d, e], s_recv.at[d, e], sibling).wait_recv()
         attend(1 - core, theirs)
 
-    @pl.loop(0, HEADS)
-    def _(h):
-        rows = pl.ds(pl.multiple_of(h * ROWS, ROWS), ROWS)
-        whole = jnp.sum(den[rows, :], axis=1, keepdims=True)
-        out_ref[h] = (acc[rows, :] / whole).astype(jnp.bfloat16)
+    out_ref[...] = (acc[...] / jnp.sum(den[...], axis=1, keepdims=True)).astype(jnp.bfloat16)
 
     rotated = page_rot[:, :ROT] + page_rot[:, ROT:]
     width = LAT + ROT
@@ -256,11 +259,15 @@
         paged_ref[:, j * width : j * width + LAT] = page_lat[rows, :].astype(jnp.bfloat16)
         paged_ref[:, j * width + LAT : (j + 1) * width] = rotated[rows, :].astype(jnp.bfloat16)
 
-    for copy in scatter + along_z + along_b + along_a:
+    for copy in scatter + along_z:
         copy.wait_send()
-    for d in range(4):
-        here = gath.at[core, (a - d + 4) % 4]
-        remote(here, here, s_send.at[d], s_recv.at[d], sibling).wait_send()
+    for e in range(4):
+        if e > 0:
+            along_b(e).wait_send()
+        for d in range(4):
+            if d > 0:
+                along_a(d, e).wait_send()
+            across(d, e).wait_send()
 
 
 def body(hidden, kv_weight, kv_gain, queries, group_order, page_owner, page_slot):
@@ -276,7 +283,7 @@
     attended, paged = pl.pallas_call(
         kernel,
         out_shape=(
-            jax.ShapeDtypeStruct((HEADS, ROWS, LAT), bf),
+            jax.ShapeDtypeStruct((rows, LAT), bf),
             jax.ShapeDtypeStruct((PAGES, 4 * (LAT + ROT)), bf),
         ),
         in_specs=[hbm, hbm, vmem, vmem, hbm, smem, vmem, vmem],
@@ -289,19 +296,20 @@
             pltpu.VMEM((7, PIECE, LAT + ROT), f32),
             pltpu.VMEM((NZ, PIECE, LAT + 128), bf),
             pltpu.VMEM((2, 4, 4, BLOCK, LAT), bf),
+            pltpu.VMEM((5, rows, 128), f32),
             pltpu.VMEM((rows, LAT), bf),
             pltpu.VMEM((rows, 128), bf),
             pltpu.VMEM((rows, LAT), f32),
             pltpu.VMEM((rows, 128), f32),
             pltpu.VMEM((rows, 128), f32),
-            pltpu.VMEM((ROWS, CHUNK), f32),
+            pltpu.VMEM((rows, 128), jnp.int32),
             pltpu.VMEM((8, CHUNK), jnp.int32),
             pltpu.VMEM((8, CHUNK), jnp.int32),
             pltpu.VMEM((ROWS, LAT), f32),
             pltpu.VMEM((ROWS, 128), f32),
             pltpu.VMEM((CHUNK, 128), bf),
-            dma((3,)), dma((7,)), dma((7,)), dma((8,)), dma((8,)), dma((4,)), dma((4,)), dma((4,)), dma((4,)),
-            dma((4,)), dma((4,)),
+            dma((3,)), dma((7,)), dma((7,)), dma((8,)), dma((8,)), dma((4,)), dma((4,)), dma((4, 4)), dma((4, 4)),
+            dma((4, 4)), dma((4, 4)),
         ],
         name="cache_attention",
         compiler_params=pltpu.CompilerParams(
@@ -312,7 +320,7 @@
         hidden, kv_weight.T, kv_gain.reshape(1, -1), jnp.asarray(freq), queries.transpose(1, 2, 0),
         group_order, page_owner, page_slot,
     )
-    return attended.transpose(1, 0, 2), paged
+    return attended.reshape(ROWS, HEADS, LAT), paged
 
 
 def solution(mesh):

time: 73.9 us -> 61.7 us (0.83)
  the two profiles are of different devices: /device:TPU:1 before, /device:TPU:65 now
where the time goes in v2:
time: 61.7 us; the launch traced here: 61.5 us
  Pallas kernels  57.9 us (94%)
  local copies, waits for them, and re-layouts  2.96 us (5%)
  between operations  0.65 us (1%)
    pallas_call x1, Pallas kernels, body(): pl.pallas_call(kernel, out_shape=(jax.ShapeDtypeStruct((rows, LAT), bf),...  57.9 us
    unnamed x4, local copies, waits for them, and re-layouts  2.96 us

profile of v2, /device:TPU:65, one launch (start us, length us, event | category | flops | bytes accessed | tf_op | source)
XLA Modules:
  0.0 61.5 jit_solution(17691498433356514279)
XLA Ops:
  0.6 57.9 %cache_attention.1 = (bf16[1024,512]{1,0:T(8,128)(2,1)}, bf16[32,2304]{1,0:T(8,128)(2,1)}) custom-call(bf16[128,896]{1,0:T(8,128)(2,1)} %hidden_hbm.1, bf16[576,896]{1,0:T(8,128)(2,1)} %bitcast.6, f32[1,512]{1,0:T(1,128)} %bitcast.7, f32[1,128]{1,0:T(1,128)} %constant.2.clone.freq_ref, bf16[8,576,128]{2,1,0:T(8,128)(2,1)} %bitcast.5, s32[64]{0:T(128)} %order_ref.1, ...), custom_call_target="tpu_custom_call" | custom-call | flops 8999999488 | bytes 4000000 | tf_op jit(solution)/shard_map/cache_attention/pallas_call | solution.py:283
  58.5 0.0 copy-start
  58.5 2.3 %copy.12 = bf16[128,8,512]{2,1,0:T(8,128)(2,1)} copy(bf16[128,8,512]{2,1,0:T(8,128)(2,1)} %bitcast.4) | data formatting | bytes 2097152
  60.8 0.0 copy-done
  60.8 0.7 %copy.13 = bf16[32,2304]{1,0:T(8,128)(2,1)} copy(bf16[32,2304]{1,0:T(8,128)(2,1)S(1)} %copy-done) | data formatting | bytes 294912
Async XLA Ops:
  58.5 2.3 %copy-start = (bf16[32,2304]{1,0:T(8,128)(2,1)S(1)}, bf16[32,2304]{1,0:T(8,128)(2,1)}, u32[]{:S(2)}) copy-start(bf16[32,2304]{1,0:T(8,128)(2,1)} %get-tuple-element.9) | copy-start | bytes 442372

commit v3 on v2

--- a/solution.py
+++ b/solution.py
@@ -36,9 +36,9 @@
 
 def kernel(
     hidden_hbm, weight_hbm, gain_ref, freq_ref, queries_hbm, order_ref, owner_ref, slot_ref,
-    out_ref, paged_ref,
-    hid, wt, qt, part, sums, zbuf, gath, q32, ql, qr, acc, top, den, qpos, kpos, drow, page_lat, page_rot, krot,
-    in_sem, rs_send, rs_recv, z_send, z_recv, b_send, b_recv, a_send, a_recv, s_send, s_recv,
+    out_hbm, paged_ref,
+    hid, wt, qt, part, sums, zbuf, gath, q32, ql, qr, acc, top, den, qpos, kpos, drow, page_lat, page_rot, krot, done,
+    in_sem, rs_send, rs_recv, z_send, z_recv, b_send, b_recv, a_send, a_recv, s_send, s_recv, out_sem,
 ):
     ctx = lax.axis_index("ctx")
     dec = lax.axis_index("dec")
@@ -53,6 +53,12 @@
     def at_ab(aa, bb):
         return device(jnp.where(first, aa, bb), jnp.where(first, bb, aa), z, core)
 
+    half_me = (x // 2 + dec % 2) % 2
+    sub_me = (x % 2) * 2 + dec % 2
+    low_at = jnp.minimum(order_ref[ctx * 2], order_ref[ctx * 2 + 1]) * HALF
+    high_at = jnp.maximum(order_ref[ctx * 2], order_ref[ctx * 2 + 1]) * HALF
+    turn = jnp.full((HALF * HEADS, LAT), order_ref[ctx * 2], jnp.int32) > order_ref[ctx * 2 + 1]
+
     rs_offsets = [(dx, dy) for dx in range(NX) for dy in range(2)][1:]
 
     def rs_device(dx, dy, sign):
@@ -60,11 +66,13 @@
         yh = (dec % 2 + dy) % 2
         return ctx, xx * 2 + yh
 
-    loads = [
-        pltpu.make_async_copy(hidden_hbm, hid, in_sem.at[0]),
-        pltpu.make_async_copy(weight_hbm, wt, in_sem.at[1]),
-        pltpu.make_async_copy(queries_hbm, qt, in_sem.at[2]),
-    ]
+    loads = [pltpu.make_async_copy(hidden_hbm, hid, in_sem.at[0])]
+    for k in range(4):
+        span = pl.ds(k * 144, 144)
+        loads.append(pltpu.make_async_copy(weight_hbm.at[span], wt.at[span], in_sem.at[1 + k]))
+    for k in range(4):
+        span = pl.ds(k * 2, 2)
+        loads.append(pltpu.make_async_copy(queries_hbm.at[span], qt.at[span], in_sem.at[5 + k]))
     for load in loads:
         load.start()
 
@@ -77,20 +85,26 @@
     for target in partners:
         pl.semaphore_signal(barrier, inc=1, device_id=target, device_id_type=MESH)
 
-    loads[0].wait()
-    loads[1].wait()
-    part[...] = lax.dot_general(
+    for load in loads[:5]:
+        load.wait()
+    projected = lax.dot_general(
         hid[...], wt[...], (((1,), (1,)), ((), ())), preferred_element_type=jnp.float32
-    ).reshape(part.shape)
+    )
+    upper, lower = projected[:HALF], projected[HALF:]
+    swap = jnp.full(upper.shape, order_ref[ctx * 2], jnp.int32) > order_ref[ctx * 2 + 1]
+    part[:4] = jnp.where(swap, lower, upper).reshape(4, PIECE, LAT + ROT)
+    part[4:] = jnp.where(swap, upper, lower).reshape(4, PIECE, LAT + ROT)
     pl.semaphore_wait(barrier, len(partners))
 
     scatter = []
     for k, (dx, dy) in enumerate(rs_offsets):
         target = rs_device(dx, dy, 1)
-        scatter.append(remote(part.at[target[1]], sums.at[k], rs_send.at[k], rs_recv.at[k], target))
+        tx, ty = target[1] // 2, target[1] % 2
+        theirs = ((tx // 2 + ty) % 2) * 4 + (tx % 2) * 2 + ty
+        scatter.append(remote(part.at[theirs], sums.at[k], rs_send.at[k], rs_recv.at[k], target))
         scatter[-1].start()
 
-    start_pos = order_ref[ctx * 2 + dec // 4] * HALF + (dec % 4) * PIECE
+    start_pos = jnp.where(half_me == 0, low_at, high_at) + sub_me * PIECE
     my_pos = (start_pos + lax.broadcasted_iota(jnp.int32, (PIECE, 128), 0)).astype(jnp.float32)
     angle = my_pos * freq_ref[...]
     cosine = jnp.cos(angle)
@@ -110,37 +124,49 @@
             picks = ctx_id == ctx_lane * 4 + (ylo * 2 + cc)
             page_z = jnp.sum(jnp.where(picks, page_of, 0.0), axis=0, keepdims=True).astype(jnp.int32)
             slot_z = jnp.sum(jnp.where(picks, slot_of, 0.0), axis=0, keepdims=True).astype(jnp.int32)
-            for xhi in range(2):
-                base = jnp.zeros((1, ROWS), jnp.int32)
-                for zz in range(NZ):
-                    base = jnp.where(lane_z == zz, order_ref[((zz * 2 + ylo) * 2 + cc) * 2 + xhi] * HALF, base)
-                for xlo in range(2):
-                    for yhi in range(2):
-                        xx, yy = xhi * 2 + xlo, yhi * 2 + ylo
-                        aa, bb = (xx, yy) if cc == 0 else (yy, xx)
-                        row, cols = cc * 4 + aa, slice(bb * ROWS, (bb + 1) * ROWS)
-                        kpos[row : row + 1, cols] = base + (xlo * 2 + yhi) * PIECE + lane_i
-                        page = (xx * 2 + yhi) * 4 + lane_i // 4
-                        drow[row : row + 1, cols] = jnp.where(page_z == page, (lane_i % 4) * PAGES + slot_z, -1)
-
-    loads[2].wait()
+            bases = [jnp.zeros((1, ROWS), jnp.int32)] * 2
+            turned = jnp.zeros((1, ROWS), jnp.int32)
+            for zz in range(NZ):
+                at = ((zz * 2 + ylo) * 2 + cc) * 2
+                one, two = order_ref[at], order_ref[at + 1]
+                bases[0] = jnp.where(lane_z == zz, jnp.minimum(one, two) * HALF, bases[0])
+                bases[1] = jnp.where(lane_z == zz, jnp.maximum(one, two) * HALF, bases[1])
+                turned = jnp.where(lane_z == zz, jnp.where(one > two, PAGES // 2, 0), turned)
+            page_z = jnp.bitwise_xor(page_z, turned)
+            for xx in range(4):
+                for yhi in range(2):
+                    aa, bb = (xx, yhi * 2 + ylo) if cc == 0 else (yhi * 2 + ylo, xx)
+                    half, sub = (xx // 2 + yhi) % 2, (xx % 2) * 2 + yhi
+                    at = (half * 2 + bb % 2) * ROWS
+                    row, cols = cc * 4 + aa, slice(at, at + ROWS)
+                    kpos[row : row + 1, cols] = bases[half] + sub * PIECE + lane_i
+                    page = half * (PAGES // 2) + sub * 4 + lane_i // 4
+                    drow[row : row + 1, cols] = jnp.where(page_z == page, (lane_i % 4) * PAGES + slot_z, -1)
+
+    for load in loads[5:]:
+        load.wait()
+    rows = HEADS * ROWS
     for h in range(HEADS):
         turned = qt[h].T.astype(jnp.float32)
         turned = jnp.concatenate([turned, turned[:, LAT:]], axis=1)
         for g in range(5):
             q32[g, pl.ds(h, ROWS, stride=HEADS), :] = turned[:, g * 128 : (g + 1) * 128]
-    for g in range(4):
-        ql[:, g * 128 : (g + 1) * 128] = q32[g].astype(jnp.bfloat16)
-    qr[...] = q32[4].astype(jnp.bfloat16)
-    token = lax.broadcasted_iota(jnp.int32, qpos.shape, 0) // HEADS
-    qpos[...] = jnp.where(token < HALF, order_ref[ctx * 2], order_ref[ctx * 2 + 1]) * HALF + token % HALF
+    for g in range(5):
+        upper, lower = q32[g, : rows // 2, :], q32[g, rows // 2 :, :]
+        swap = turn[:, :128]
+        ordered = jnp.concatenate([jnp.where(swap, lower, upper), jnp.where(swap, upper, lower)], axis=0)
+        if g < 4:
+            ql[:, g * 128 : (g + 1) * 128] = ordered.astype(jnp.bfloat16)
+        else:
+            qr[...] = ordered.astype(jnp.bfloat16)
+    qpos[...] = lax.broadcasted_iota(jnp.int32, qpos.shape, 0) // HEADS
     acc[...] = jnp.zeros_like(acc)
     den[...] = jnp.zeros_like(den)
     top[...] = jnp.full_like(top, NEG)
     page_lat[...] = jnp.zeros_like(page_lat)
     page_rot[...] = jnp.zeros_like(page_rot)
 
-    total = part[dec]
+    total = part[half_me * 4 + sub_me]
     for k, copy in enumerate(scatter):
         copy.wait_recv()
         total = total + sums[k]
@@ -187,87 +213,167 @@
     def across(d, e):
         return remote(block(d, e), block(d, e), s_send.at[d, e], s_recv.at[d, e], sibling)
 
+    def onward(e):
+        came, to = (block(1, e), a + 1) if e in (0, 1) else (block(3, e), a + 3)
+        return remote(came, came, a_send.at[2, e], a_recv.at[2, e], at_ab(to % 4, b))
+
+    def arrived(d, e):
+        came = block(d, e)
+        remote(came, came, a_send.at[d, e], a_recv.at[d, e], at_ab((a + d) % 4, b)).wait_recv()
+
+    def take(d, e):
+        arrived(d, e)
+        if (d, e) in ((1, 0), (1, 1), (3, 2), (3, 3)):
+            onward(e).start()
+        across(d, e).start()
+
     for e in (1, 3, 2):
         along_b(e).start()
     for e in (0, 1, 3, 2):
         if e > 0:
             came = block(0, e)
             remote(came, came, b_send.at[e], b_recv.at[e], at_ab(a, (b + e) % 4)).wait_recv()
-        for d in (1, 3, 2):
+        for d in (1, 3):
             along_a(d, e).start()
         across(0, e).start()
+        if e == 3:
+            take(1, 0)
+            take(3, 0)
 
     page_row = lax.broadcasted_iota(jnp.int32, (ROWS, CHUNK), 0)
 
     def attend(cc, aa):
         which = cc * 4 + aa
         pick = jnp.where(drow[pl.ds(which, 1), :] == page_row, 1.0, 0.0).astype(jnp.bfloat16)
-        for bb in range(4):
+        same = (aa // 2) * 2
+        order = (same, same + 1, 2 - same, 3 - same)
+        for at, bb in enumerate(order):
             for zz in range(NZ):
                 rot = gath[cc, aa, bb, ROWS:, (zz // 2) * 128 : (zz // 2 + 1) * 128]
                 keep = left if zz % 2 == 0 else jnp.logical_not(left)
-                krot[bb * ROWS + zz * PIECE : bb * ROWS + (zz + 1) * PIECE, :] = jnp.where(
+                krot[at * ROWS + zz * PIECE : at * ROWS + (zz + 1) * PIECE, :] = jnp.where(
                     keep, rot, jnp.zeros_like(rot)
                 )
 
-        def keys():
-            return jnp.concatenate([gath[cc, aa, bb, :ROWS, :] for bb in range(4)], axis=0)
+        def keys(count=4):
+            return jnp.concatenate([gath[cc, aa, bb, :ROWS, :] for bb in order[:count]], axis=0)
 
         page_lat[...] += jnp.dot(pick, keys(), preferred_element_type=jnp.float32)
         page_rot[...] += jnp.dot(pick, krot[...], preferred_element_type=jnp.float32)
 
         nt = (((1,), (1,)), ((), ()))
-        scores = lax.dot_general(ql[...], keys(), nt, preferred_element_type=jnp.float32)
-        scores += lax.dot_general(qr[...], krot[...], nt, preferred_element_type=jnp.float32)
-        limit = jnp.concatenate([qpos[...]] * 4, axis=1)
-        scores = jnp.where(kpos[pl.ds(which, 1), :] <= limit, scores, NEG)
-        old = top[...]
-        new = jnp.maximum(old, jnp.max(scores, axis=1, keepdims=True))
-        alpha = jnp.exp2((old - new) * LOG2E_SCALE)
-        weights = jnp.exp2((scores - jnp.concatenate([new] * 4, axis=1)) * LOG2E_SCALE)
-        top[...] = new
-        den[...] = den[...] * alpha + (
-            (weights[:, :128] + weights[:, 128:256]) + (weights[:, 256:384] + weights[:, 384:])
+        kp = kpos[pl.ds(which, 1), :]
+        near = CHUNK // 2
+
+        def logits(rows, count):
+            scores = lax.dot_general(ql[rows, :], keys(count), nt, preferred_element_type=jnp.float32)
+            return scores + lax.dot_general(
+                qr[rows, :], krot[: count * ROWS, :], nt, preferred_element_type=jnp.float32
+            )
+
+        def fold(rows, scores, count):
+            old = top[rows, :]
+            new = jnp.maximum(old, jnp.max(scores, axis=1, keepdims=True))
+            alpha = jnp.exp2((old - new) * LOG2E_SCALE)
+            weights = jnp.exp2((scores - jnp.concatenate([new] * count, axis=1)) * LOG2E_SCALE)
+            top[rows, :] = new
+            summed = weights[:, :128]
+            for part_at in range(1, count):
+                summed += weights[:, part_at * 128 : (part_at + 1) * 128]
+            den[rows, :] = den[rows, :] * alpha + summed
+            mixed = jnp.dot(weights.astype(jnp.bfloat16), keys(count), preferred_element_type=jnp.float32)
+            acc[rows, :] = acc[rows, :] * jnp.concatenate([alpha] * 4, axis=1) + mixed
+
+        low_rows, high_rows = slice(0, HALF * HEADS), slice(HALF * HEADS, 2 * HALF * HEADS)
+        limit = jnp.concatenate([qpos[...]] * 2, axis=1)
+        high = logits(high_rows, 4)
+        low = logits(low_rows, 2)
+        high = jnp.concatenate(
+            [high[:, :near], jnp.where(kp[:, near:] - high_at <= limit, high[:, near:], NEG)], axis=1
         )
-        mixed = jnp.dot(weights.astype(jnp.bfloat16), keys(), preferred_element_type=jnp.float32)
-        acc[...] = acc[...] * jnp.concatenate([alpha] * 4, axis=1) + mixed
+        low = jnp.where(kp[:, :near] - low_at <= limit, low, NEG)
+        fold(high_rows, high, 4)
+        fold(low_rows, low, 2)
 
     @pl.loop(0, 4)
     def _(k):
         d = k ^ (k // 2)
 
-        @pl.when(k > 0)
+        @pl.when(k == 3)
         def _():
             for e in (0, 1, 3, 2):
-                came = block(d, e)
-                remote(came, came, a_send.at[d, e], a_recv.at[d, e], at_ab((a + d) % 4, b)).wait_recv()
-                across(d, e).start()
+                arrived(2, e)
+                across(2, e).start()
 
         attend(core, (a - d + 4) % 4)
+
+        @pl.when(k == 0)
+        def _():
+            take(1, 1)
+            take(3, 3)
+
         theirs = (b - d + 4) % 4
         for e in (0, 1, 3, 2):
             there = gath.at[1 - core, theirs, (a - e + 4) % 4]
             remote(there, there, s_send.at[d, e], s_recv.at[d, e], sibling).wait_recv()
         attend(1 - core, theirs)
 
-    out_ref[...] = (acc[...] / jnp.sum(den[...], axis=1, keepdims=True)).astype(jnp.bfloat16)
+        @pl.when(k == 0)
+        def _():
+            take(3, 2)
+            take(1, 3)
+            take(1, 2)
+            take(3, 1)
+
+    leaving = []
+    for k in range(4):
+        low_span, high_span = slice(k * ROWS, (k + 1) * ROWS), slice((k + 4) * ROWS, (k + 5) * ROWS)
+        low = acc[low_span, :] / jnp.sum(den[low_span, :], axis=1, keepdims=True)
+        high = acc[high_span, :] / jnp.sum(den[high_span, :], axis=1, keepdims=True)
+        swap = turn[:ROWS]
+        done[low_span, :] = jnp.where(swap, high, low).astype(jnp.bfloat16)
+        done[high_span, :] = jnp.where(swap, low, high).astype(jnp.bfloat16)
+        for at in (k, k + 4):
+            span = pl.ds(at * ROWS, ROWS)
+            leaving.append(pltpu.make_async_copy(done.at[span], out_hbm.at[span], out_sem.at[at]))
+            leaving[-1].start()
 
     rotated = page_rot[:, :ROT] + page_rot[:, ROT:]
     width = LAT + ROT
     for j in range(4):
-        rows = slice(j * PAGES, (j + 1) * PAGES)
-        paged_ref[:, j * width : j * width + LAT] = page_lat[rows, :].astype(jnp.bfloat16)
-        paged_ref[:, j * width + LAT : (j + 1) * width] = rotated[rows, :].astype(jnp.bfloat16)
-
+        span = slice(j * PAGES, (j + 1) * PAGES)
+        paged_ref[:, j * width : j * width + LAT] = page_lat[span, :].astype(jnp.bfloat16)
+        paged_ref[:, j * width + LAT : (j + 1) * width] = rotated[span, :].astype(jnp.bfloat16)
+
+    for copy in leaving:
+        copy.wait()
     for copy in scatter + along_z:
         copy.wait_send()
     for e in range(4):
         if e > 0:
             along_b(e).wait_send()
+        for d in (1, 3):
+            along_a(d, e).wait_send()
+        onward(e).wait_send()
         for d in range(4):
-            if d > 0:
-                along_a(d, e).wait_send()
             across(d, e).wait_send()
+
+
+def place(attended_hbm, paged_hbm, out_hbm, paged_out_hbm, held, paged_held, in_sem, out_sem):
+    pairs = []
+    for k in range(8):
+        span = pl.ds(k * ROWS, ROWS)
+        pairs.append((attended_hbm.at[span], held.at[span], out_hbm.at[span]))
+    pairs.append((paged_hbm, paged_held, paged_out_hbm))
+    come = [pltpu.make_async_copy(p[0], p[1], in_sem.at[k]) for k, p in enumerate(pairs)]
+    go = [pltpu.make_async_copy(p[1], p[2], out_sem.at[k]) for k, p in enumerate(pairs)]
+    for copy in come:
+        copy.start()
+    for first, second in zip(come, go):
+        first.wait()
+        second.start()
+    for copy in go:
+        copy.wait()
 
 
 def body(hidden, kv_weight, kv_gain, queries, group_order, page_owner, page_slot):
@@ -287,7 +393,7 @@
             jax.ShapeDtypeStruct((PAGES, 4 * (LAT + ROT)), bf),
         ),
         in_specs=[hbm, hbm, vmem, vmem, hbm, smem, vmem, vmem],
-        out_specs=(vmem, vmem),
+        out_specs=(hbm, vmem),
         scratch_shapes=[
             pltpu.VMEM(hidden.shape, bf),
             pltpu.VMEM(kv_weight.shape[::-1], bf),
@@ -302,14 +408,15 @@
             pltpu.VMEM((rows, LAT), f32),
             pltpu.VMEM((rows, 128), f32),
             pltpu.VMEM((rows, 128), f32),
-            pltpu.VMEM((rows, 128), jnp.int32),
+            pltpu.VMEM((rows // 2, 128), jnp.int32),
             pltpu.VMEM((8, CHUNK), jnp.int32),
             pltpu.VMEM((8, CHUNK), jnp.int32),
             pltpu.VMEM((ROWS, LAT), f32),
             pltpu.VMEM((ROWS, 128), f32),
             pltpu.VMEM((CHUNK, 128), bf),
-            dma((3,)), dma((7,)), dma((7,)), dma((8,)), dma((8,)), dma((4,)), dma((4,)), dma((4, 4)), dma((4, 4)),
-            dma((4, 4)), dma((4, 4)),
+            pltpu.VMEM((rows, LAT), bf),
+            dma((9,)), dma((7,)), dma((7,)), dma((8,)), dma((8,)), dma((4,)), dma((4,)), dma((4, 4)), dma((4, 4)),
+            dma((4, 4)), dma((4, 4)), dma((8,)),
         ],
         name="cache_attention",
         compiler_params=pltpu.CompilerParams(
@@ -320,6 +427,18 @@
         hidden, kv_weight.T, kv_gain.reshape(1, -1), jnp.asarray(freq), queries.transpose(1, 2, 0),
         group_order, page_owner, page_slot,
     )
+    attended, paged = pl.pallas_call(
+        place,
+        out_shape=(
+            jax.ShapeDtypeStruct(attended.shape, bf),
+            jax.ShapeDtypeStruct(paged.shape, bf),
+        ),
+        in_specs=[hbm, hbm],
+        out_specs=(hbm, hbm),
+        scratch_shapes=[pltpu.VMEM(attended.shape, bf), pltpu.VMEM(paged.shape, bf), dma((9,)), dma((9,))],
+        compiler_params=pltpu.CompilerParams(vmem_limit_bytes=56 * 2**20),
+        name="place",
+    )(attended, paged)
     return attended.reshape(ROWS, HEADS, LAT), paged
 
 

time: 61.7 us -> 56.7 us (0.919)
  the two profiles are of different devices: /device:TPU:65 before, /device:TPU:1 now
where the time goes in v3:
time: 56.7 us; the launch traced here: 56.5 us
  Pallas kernels  55.8 us (98%)
  between operations  0.64 us (1%)
    pallas_call x1, Pallas kernels, body(): pl.pallas_call(kernel, out_shape=(jax.ShapeDtypeStruct((rows, LAT), bf),...  53.7 us
    pallas_call x1, Pallas kernels, body(): pl.pallas_call(place, out_shape=(jax.ShapeDtypeStruct(attended.shape, bf)...  2.15 us

profile of v3, /device:TPU:1, one launch (start us, length us, event | category | flops | bytes accessed | tf_op | source)
XLA Modules:
  0.0 56.5 jit_solution(8709131632153501643)
XLA Ops:
  0.6 53.7 %cache_attention.1 = (bf16[1024,512]{1,0:T(8,128)(2,1)}, bf16[32,2304]{1,0:T(8,128)(2,1)}) custom-call(bf16[128,896]{1,0:T(8,128)(2,1)} %hidden_hbm.1, bf16[576,896]{1,0:T(8,128)(2,1)} %bitcast.6, f32[1,512]{1,0:T(1,128)} %bitcast.7, f32[1,128]{1,0:T(1,128)} %constant.2.clone.freq_ref, bf16[8,576,128]{2,1,0:T(8,128)(2,1)} %bitcast.4, s32[64]{0:T(128)} %order_ref.1, ...), custom_call_target="tpu_custom_call" | custom-call | flops 8999999488 | bytes 4000000 | tf_op jit(solution)/shard_map/cache_attention/pallas_call | solution.py:389
  54.3 2.2 %place.1 = (bf16[1024,512]{1,0:T(8,128)(2,1)}, bf16[32,2304]{1,0:T(8,128)(2,1)}) custom-call(bf16[1024,512]{1,0:T(8,128)(2,1)} %get-tuple-element.6.attended_hbm, bf16[32,2304]{1,0:T(8,128)(2,1)} %get-tuple-element.7.paged_hbm), custom_call_target="tpu_custom_call" | custom-call | tf_op jit(solution)/shard_map/place/pallas_call | solution.py:430

commit v4 on v3

--- a/solution.py
+++ b/solution.py
@@ -36,9 +36,9 @@
 
 def kernel(
     hidden_hbm, weight_hbm, gain_ref, freq_ref, queries_hbm, order_ref, owner_ref, slot_ref,
-    out_hbm, paged_ref,
-    hid, wt, qt, part, sums, zbuf, gath, q32, ql, qr, acc, top, den, qpos, kpos, drow, page_lat, page_rot, krot, done,
-    in_sem, rs_send, rs_recv, z_send, z_recv, b_send, b_recv, a_send, a_recv, s_send, s_recv, out_sem,
+    out_ref, paged_ref,
+    hid, wt, qt, part, sums, zbuf, gath, q32, ql, qr, acc, top, den, qpos, kpos, drow, page_lat, page_rot, krot,
+    in_sem, rs_send, rs_recv, z_send, z_recv, b_send, b_recv, a_send, a_recv, s_send, s_recv,
 ):
     ctx = lax.axis_index("ctx")
     dec = lax.axis_index("dec")
@@ -59,7 +59,7 @@
     high_at = jnp.maximum(order_ref[ctx * 2], order_ref[ctx * 2 + 1]) * HALF
     turn = jnp.full((HALF * HEADS, LAT), order_ref[ctx * 2], jnp.int32) > order_ref[ctx * 2 + 1]
 
-    rs_offsets = [(dx, dy) for dx in range(NX) for dy in range(2)][1:]
+    rs_offsets = [(2, 1), (1, 1), (3, 1), (2, 0), (0, 1), (1, 0), (3, 0)]
 
     def rs_device(dx, dy, sign):
         xx = (x + sign * dx + NX) % NX
@@ -137,11 +137,10 @@
                 for yhi in range(2):
                     aa, bb = (xx, yhi * 2 + ylo) if cc == 0 else (yhi * 2 + ylo, xx)
                     half, sub = (xx // 2 + yhi) % 2, (xx % 2) * 2 + yhi
-                    at = (half * 2 + bb % 2) * ROWS
-                    row, cols = cc * 4 + aa, slice(at, at + ROWS)
-                    kpos[row : row + 1, cols] = bases[half] + sub * PIECE + lane_i
+                    row = (cc * 4 + aa) * 4 + bb
+                    kpos[row : row + 1, :] = bases[half] + sub * PIECE + lane_i
                     page = half * (PAGES // 2) + sub * 4 + lane_i // 4
-                    drow[row : row + 1, cols] = jnp.where(page_z == page, (lane_i % 4) * PAGES + slot_z, -1)
+                    drow[row : row + 1, :] = jnp.where(page_z == page, (lane_i % 4) * PAGES + slot_z, -1)
 
     for load in loads[5:]:
         load.wait()
@@ -181,7 +180,7 @@
     zbuf[z] = jnp.concatenate([latent, turned, turned], axis=1).astype(jnp.bfloat16)
 
     along_z = []
-    for dz in range(1, NZ):
+    for dz in (4, 3, 5, 2, 6, 1, 7):
         copy = remote(zbuf.at[z], zbuf.at[z], z_send.at[dz], z_recv.at[dz], device(x, y, (z + dz) % NZ, core))
         copy.start()
         along_z.append(copy)
@@ -242,12 +241,20 @@
 
     page_row = lax.broadcasted_iota(jnp.int32, (ROWS, CHUNK), 0)
 
-    def attend(cc, aa):
-        which = cc * 4 + aa
-        pick = jnp.where(drow[pl.ds(which, 1), :] == page_row, 1.0, 0.0).astype(jnp.bfloat16)
-        same = (aa // 2) * 2
-        order = (same, same + 1, 2 - same, 3 - same)
-        for at, bb in enumerate(order):
+    def attend(cc, pa, pb, k):
+        near = jnp.logical_or(k == 1, k == 2)
+        strip = (pa + jnp.where(k == 3, 2, 0)) % 4
+        order = []
+        for at in range(4):
+            bb_near = (pb - 2 * (k - 1) - at % 2 + 8) % 4
+            half = bb_near // 2 if at < 2 else 1 - bb_near // 2
+            aa_near = half * 2 + (pa + 1) % 2
+            bb_strip = (strip // 2 if at < 2 else 1 - strip // 2) * 2 + at % 2
+            order.append((jnp.where(near, aa_near, strip), jnp.where(near, bb_near, bb_strip)))
+        which = [(cc * 4 + aa) * 4 + bb for aa, bb in order]
+        row_of = jnp.concatenate([drow[pl.ds(w, 1), :] for w in which], axis=1)
+        pick = jnp.where(row_of == page_row, 1.0, 0.0).astype(jnp.bfloat16)
+        for at, (aa, bb) in enumerate(order):
             for zz in range(NZ):
                 rot = gath[cc, aa, bb, ROWS:, (zz // 2) * 128 : (zz // 2 + 1) * 128]
                 keep = left if zz % 2 == 0 else jnp.logical_not(left)
@@ -256,13 +263,13 @@
                 )
 
         def keys(count=4):
-            return jnp.concatenate([gath[cc, aa, bb, :ROWS, :] for bb in order[:count]], axis=0)
+            return jnp.concatenate([gath[cc, aa, bb, :ROWS, :] for aa, bb in order[:count]], axis=0)
 
         page_lat[...] += jnp.dot(pick, keys(), preferred_element_type=jnp.float32)
         page_rot[...] += jnp.dot(pick, krot[...], preferred_element_type=jnp.float32)
 
         nt = (((1,), (1,)), ((), ()))
-        kp = kpos[pl.ds(which, 1), :]
+        kp = jnp.concatenate([kpos[pl.ds(w, 1), :] for w in which], axis=1)
         near = CHUNK // 2
 
         def logits(rows, count):
@@ -297,46 +304,45 @@
 
     @pl.loop(0, 4)
     def _(k):
-        d = k ^ (k // 2)
-
         @pl.when(k == 3)
         def _():
-            for e in (0, 1, 3, 2):
+            for e in (3, 2):
                 arrived(2, e)
                 across(2, e).start()
 
-        attend(core, (a - d + 4) % 4)
+        attend(core, a, b, k)
 
         @pl.when(k == 0)
         def _():
-            take(1, 1)
-            take(3, 3)
-
-        theirs = (b - d + 4) % 4
-        for e in (0, 1, 3, 2):
-            there = gath.at[1 - core, theirs, (a - e + 4) % 4]
+            for d, e in ((1, 1), (3, 1), (3, 3), (1, 3)):
+                take(d, e)
+
+        @pl.when(k == 1)
+        def _():
+            for d, e in ((3, 2), (1, 2)):
+                take(d, e)
+
+        @pl.when(k == 2)
+        def _():
+            for e in (0, 1):
+                arrived(2, e)
+                across(2, e).start()
+
+        near = jnp.logical_or(k == 1, k == 2)
+        for at in range(4):
+            d = jnp.where(near, 1 + 2 * (at % 2), jnp.where(k == 3, 2, 0))
+            e = jnp.where(near, jnp.where(k == 1, at // 2, 3 - at // 2), at)
+            there = gath.at[1 - core, (b - d + 4) % 4, (a - e + 4) % 4]
             remote(there, there, s_send.at[d, e], s_recv.at[d, e], sibling).wait_recv()
-        attend(1 - core, theirs)
-
-        @pl.when(k == 0)
-        def _():
-            take(3, 2)
-            take(1, 3)
-            take(1, 2)
-            take(3, 1)
-
-    leaving = []
+        attend(1 - core, b, a, k)
+
     for k in range(4):
         low_span, high_span = slice(k * ROWS, (k + 1) * ROWS), slice((k + 4) * ROWS, (k + 5) * ROWS)
         low = acc[low_span, :] / jnp.sum(den[low_span, :], axis=1, keepdims=True)
         high = acc[high_span, :] / jnp.sum(den[high_span, :], axis=1, keepdims=True)
         swap = turn[:ROWS]
-        done[low_span, :] = jnp.where(swap, high, low).astype(jnp.bfloat16)
-        done[high_span, :] = jnp.where(swap, low, high).astype(jnp.bfloat16)
-        for at in (k, k + 4):
-            span = pl.ds(at * ROWS, ROWS)
-            leaving.append(pltpu.make_async_copy(done.at[span], out_hbm.at[span], out_sem.at[at]))
-            leaving[-1].start()
+        out_ref[low_span, :] = jnp.where(swap, high, low).astype(jnp.bfloat16)
+        out_ref[high_span, :] = jnp.where(swap, low, high).astype(jnp.bfloat16)
 
     rotated = page_rot[:, :ROT] + page_rot[:, ROT:]
     width = LAT + ROT
@@ -345,8 +351,6 @@
         paged_ref[:, j * width : j * width + LAT] = page_lat[span, :].astype(jnp.bfloat16)
         paged_ref[:, j * width + LAT : (j + 1) * width] = rotated[span, :].astype(jnp.bfloat16)
 
-    for copy in leaving:
-        copy.wait()
     for copy in scatter + along_z:
         copy.wait_send()
     for e in range(4):
@@ -357,23 +361,6 @@
         onward(e).wait_send()
         for d in range(4):
             across(d, e).wait_send()
-
-
-def place(attended_hbm, paged_hbm, out_hbm, paged_out_hbm, held, paged_held, in_sem, out_sem):
-    pairs = []
-    for k in range(8):
-        span = pl.ds(k * ROWS, ROWS)
-        pairs.append((attended_hbm.at[span], held.at[span], out_hbm.at[span]))
-    pairs.append((paged_hbm, paged_held, paged_out_hbm))
-    come = [pltpu.make_async_copy(p[0], p[1], in_sem.at[k]) for k, p in enumerate(pairs)]
-    go = [pltpu.make_async_copy(p[1], p[2], out_sem.at[k]) for k, p in enumerate(pairs)]
-    for copy in come:
-        copy.start()
-    for first, second in zip(come, go):
-        first.wait()
-        second.start()
-    for copy in go:
-        copy.wait()
 
 
 def body(hidden, kv_weight, kv_gain, queries, group_order, page_owner, page_slot):
@@ -389,11 +376,11 @@
     attended, paged = pl.pallas_call(
         kernel,
         out_shape=(
-            jax.ShapeDtypeStruct((rows, LAT), bf),
-            jax.ShapeDtypeStruct((PAGES, 4 * (LAT + ROT)), bf),
+            pltpu.VMEM((rows, LAT), bf),
+            pltpu.VMEM((PAGES, 4 * (LAT + ROT)), bf),
         ),
         in_specs=[hbm, hbm, vmem, vmem, hbm, smem, vmem, vmem],
-        out_specs=(hbm, vmem),
+        out_specs=(vmem, vmem),
         scratch_shapes=[
             pltpu.VMEM(hidden.shape, bf),
             pltpu.VMEM(kv_weight.shape[::-1], bf),
@@ -409,14 +396,13 @@
             pltpu.VMEM((rows, 128), f32),
             pltpu.VMEM((rows, 128), f32),
             pltpu.VMEM((rows // 2, 128), jnp.int32),
-            pltpu.VMEM((8, CHUNK), jnp.int32),
-            pltpu.VMEM((8, CHUNK), jnp.int32),
+            pltpu.VMEM((32, ROWS), jnp.int32),
+            pltpu.VMEM((32, ROWS), jnp.int32),
             pltpu.VMEM((ROWS, LAT), f32),
             pltpu.VMEM((ROWS, 128), f32),
             pltpu.VMEM((CHUNK, 128), bf),
-            pltpu.VMEM((rows, LAT), bf),
             dma((9,)), dma((7,)), dma((7,)), dma((8,)), dma((8,)), dma((4,)), dma((4,)), dma((4, 4)), dma((4, 4)),
-            dma((4, 4)), dma((4, 4)), dma((8,)),
+            dma((4, 4)), dma((4, 4)),
         ],
         name="cache_attention",
         compiler_params=pltpu.CompilerParams(
@@ -427,18 +413,6 @@
         hidden, kv_weight.T, kv_gain.reshape(1, -1), jnp.asarray(freq), queries.transpose(1, 2, 0),
         group_order, page_owner, page_slot,
     )
-    attended, paged = pl.pallas_call(
-        place,
-        out_shape=(
-            jax.ShapeDtypeStruct(attended.shape, bf),
-            jax.ShapeDtypeStruct(paged.shape, bf),
-        ),
-        in_specs=[hbm, hbm],
-        out_specs=(hbm, hbm),
-        scratch_shapes=[pltpu.VMEM(attended.shape, bf), pltpu.VMEM(paged.shape, bf), dma((9,)), dma((9,))],
-        compiler_params=pltpu.CompilerParams(vmem_limit_bytes=56 * 2**20),
-        name="place",
-    )(attended, paged)
     return attended.reshape(ROWS, HEADS, LAT), paged
 
 

time: 56.7 us -> 50.3 us (0.89)
  Pallas kernels: 55.8 us -> 47.9 us
  local copies, waits for them, and re-layouts: 0 us -> 1.63 us
    pallas_call x2 -> x1, Pallas kernels: 55.8 us -> 47.9 us  [body(): pl.pallas_call(kernel, out_shape=(pltpu.VMEM((rows, LAT), bf), pltpu.VMEM...]
    unnamed x0 -> x2, local copies, waits for them, and re-layouts: none -> 1.63 us
where the time goes in v4:
time: 50.3 us; the launch traced here: 50.2 us
  Pallas kernels  47.9 us (95%)
  local copies, waits for them, and re-layouts  1.63 us (3%)
  between operations  0.64 us (1%)
    pallas_call x1, Pallas kernels, body(): pl.pallas_call(kernel, out_shape=(pltpu.VMEM((rows, LAT), bf), pltpu.VMEM...  47.9 us
    unnamed x2, local copies, waits for them, and re-layouts  1.63 us

profile of v4, /device:TPU:1, one launch (start us, length us, event | category | flops | bytes accessed | tf_op | source)
XLA Modules:
  0.0 50.2 jit_solution(9396701894139020851)
XLA Ops:
  0.6 47.9 %cache_attention.1 = (bf16[1024,512]{1,0:T(8,128)(2,1)S(1)}, bf16[32,2304]{1,0:T(8,128)(2,1)S(1)}) custom-call(bf16[128,896]{1,0:T(8,128)(2,1)} %hidden_hbm.1, bf16[576,896]{1,0:T(8,128)(2,1)} %bitcast.6, f32[1,512]{1,0:T(1,128)} %bitcast.7, f32[1,128]{1,0:T(1,128)} %constant.2.clone.freq_ref, bf16[8,576,128]{2,1,0:T(8,128)(2,1)} %bitcast.5, s32[64]{0:T(128)} %order_ref.1, ...), custom_call_target="tpu_custom_call" | custom-call | flops 8999999488 | bytes 4000000 | tf_op jit(solution)/shard_map/cache_attention/pallas_call | solution.py:376
  48.5 1.0 %copy.12 = bf16[128,8,512]{2,1,0:T(8,128)(2,1)} copy(bf16[128,8,512]{2,1,0:T(8,128)(2,1)S(1)} %bitcast.4) | data formatting | bytes 2097152
  49.5 0.7 %copy.13 = bf16[32,2304]{1,0:T(8,128)(2,1)} copy(bf16[32,2304]{1,0:T(8,128)(2,1)S(1)} %get-tuple-element.7) | data formatting | bytes 294912

commit v5 on v4

--- a/solution.py
+++ b/solution.py
@@ -22,6 +22,8 @@
 EPS = 1e-6
 LOG2E_SCALE = float(192.0 ** (-0.5) * np.log2(np.e))
 NEG = -1e30
+STEPS = (0, 1, 7, 2, 6, 3, 5, 4)
+EARLY = ROWS // 2
 
 
 def device(x, y, z, core):
@@ -118,7 +120,10 @@
     page_of = jnp.sum(jnp.where(mine, page_id, 0.0), axis=1, keepdims=True)
     slot_of = jnp.sum(jnp.where(mine, slot_ref[...].astype(jnp.float32), 0.0), axis=1, keepdims=True)
     ctx_id = lax.broadcasted_iota(jnp.int32, (PAGES, ROWS), 0)
-    ctx_lane = lax.broadcasted_iota(jnp.int32, (PAGES, ROWS), 1) // PIECE
+    place_lane = lax.broadcasted_iota(jnp.int32, (PAGES, ROWS), 1) // PIECE
+    ctx_lane = jnp.zeros((PAGES, ROWS), jnp.int32)
+    for at, step in enumerate(STEPS):
+        ctx_lane = jnp.where(place_lane == at, (z + step) % NZ, ctx_lane)
     for cc in range(2):
         for ylo in range(2):
             picks = ctx_id == ctx_lane * 4 + (ylo * 2 + cc)
@@ -126,8 +131,8 @@
             slot_z = jnp.sum(jnp.where(picks, slot_of, 0.0), axis=0, keepdims=True).astype(jnp.int32)
             bases = [jnp.zeros((1, ROWS), jnp.int32)] * 2
             turned = jnp.zeros((1, ROWS), jnp.int32)
-            for zz in range(NZ):
-                at = ((zz * 2 + ylo) * 2 + cc) * 2
+            for zz, step in enumerate(STEPS):
+                at = (((z + step) % NZ * 2 + ylo) * 2 + cc) * 2
                 one, two = order_ref[at], order_ref[at + 1]
                 bases[0] = jnp.where(lane_z == zz, jnp.minimum(one, two) * HALF, bases[0])
                 bases[1] = jnp.where(lane_z == zz, jnp.maximum(one, two) * HALF, bases[1])
@@ -180,31 +185,40 @@
     zbuf[z] = jnp.concatenate([latent, turned, turned], axis=1).astype(jnp.bfloat16)
 
     along_z = []
-    for dz in (4, 3, 5, 2, 6, 1, 7):
+    for dz in (7, 1, 6, 4, 3, 5, 2):
         copy = remote(zbuf.at[z], zbuf.at[z], z_send.at[dz], z_recv.at[dz], device(x, y, (z + dz) % NZ, core))
         copy.start()
         along_z.append(copy)
-    for dz in range(1, NZ):
-        came = (z - dz + NZ) % NZ
-        remote(
-            zbuf.at[came], zbuf.at[came], z_send.at[dz], z_recv.at[dz], device(x, y, (z + dz) % NZ, core)
-        ).wait_recv()
     left = lax.broadcasted_iota(jnp.int32, (PIECE, 128), 1) < ROT
     mine_block = gath.at[core, a, b]
-    for zz in range(NZ):
-        mine_block[zz * PIECE : (zz + 1) * PIECE, :] = zbuf[zz, :, :LAT]
-    for pair in range(NZ // 2):
-        mine_block[ROWS:, pair * 128 : (pair + 1) * 128] = jnp.where(
-            left, zbuf[2 * pair, :, LAT:], zbuf[2 * pair + 1, :, LAT:]
-        )
+
+    def settle(places):
+        for at in places:
+            came = (z + STEPS[at]) % NZ
+            dz = (NZ - STEPS[at]) % NZ
+            if dz > 0:
+                remote(
+                    zbuf.at[came], zbuf.at[came], z_send.at[dz], z_recv.at[dz], device(x, y, (z + dz) % NZ, core)
+                ).wait_recv()
+        for at in places:
+            mine_block[at * PIECE : (at + 1) * PIECE, :] = zbuf[(z + STEPS[at]) % NZ, :, :LAT]
 
     sibling = device(x, y, z, 1 - core)
 
     def block(d, e):
         return gath.at[core, (a - d + 4) % 4, (b - e + 4) % 4]
 
-    def along_b(e):
-        return remote(mine_block, mine_block, b_send.at[e], b_recv.at[e], at_ab(a, (b + e) % 4))
+    def some(ref, h):
+        return ref.at[pl.ds(0, EARLY)] if h == 0 else ref.at[pl.ds(EARLY, BLOCK - EARLY)]
+
+    def along_b(e, h):
+        return remote(some(mine_block, h), some(mine_block, h), b_send.at[e, h], b_recv.at[e, h], at_ab(a, (b + e) % 4))
+
+    def own_along_a(d, h):
+        col = 4 * (1 - h)
+        return remote(
+            some(mine_block, h), some(mine_block, h), a_send.at[d, col], a_recv.at[d, col], at_ab((a + d) % 4, b)
+        )
 
     def along_a(d, e):
         return remote(block(0, e), block(0, e), a_send.at[d, e], a_recv.at[d, e], at_ab((a + d) % 4, b))
@@ -218,7 +232,14 @@
 
     def arrived(d, e):
         came = block(d, e)
-        remote(came, came, a_send.at[d, e], a_recv.at[d, e], at_ab((a + d) % 4, b)).wait_recv()
+        if e == 0 and d != 2:
+            for h in range(2):
+                col = 4 * (1 - h)
+                remote(
+                    some(came, h), some(came, h), a_send.at[d, col], a_recv.at[d, col], at_ab((a + d) % 4, b)
+                ).wait_recv()
+        else:
+            remote(came, came, a_send.at[d, e], a_recv.at[d, e], at_ab((a + d) % 4, b)).wait_recv()
 
     def take(d, e):
         arrived(d, e)
@@ -226,14 +247,26 @@
             onward(e).start()
         across(d, e).start()
 
-    for e in (1, 3, 2):
-        along_b(e).start()
+    for h in range(2):
+        settle(range(4 * h, 4 * h + 4))
+        if h == 1:
+            for pair in range(NZ // 2):
+                mine_block[ROWS:, pair * 128 : (pair + 1) * 128] = jnp.where(
+                    left,
+                    zbuf[(z + STEPS[2 * pair]) % NZ, :, LAT:],
+                    zbuf[(z + STEPS[2 * pair + 1]) % NZ, :, LAT:],
+                )
+        for e in (1, 3, 2):
+            along_b(e, h).start()
+        for d in (1, 3):
+            own_along_a(d, h).start()
     for e in (0, 1, 3, 2):
         if e > 0:
-            came = block(0, e)
-            remote(came, came, b_send.at[e], b_recv.at[e], at_ab(a, (b + e) % 4)).wait_recv()
-        for d in (1, 3):
-            along_a(d, e).start()
+            for h in range(2):
+                came = some(block(0, e), h)
+                remote(came, came, b_send.at[e, h], b_recv.at[e, h], at_ab(a, (b + e) % 4)).wait_recv()
+            for d in (1, 3):
+                along_a(d, e).start()
         across(0, e).start()
         if e == 3:
             take(1, 0)
@@ -355,9 +388,14 @@
         copy.wait_send()
     for e in range(4):
         if e > 0:
-            along_b(e).wait_send()
+            for h in range(2):
+                along_b(e, h).wait_send()
         for d in (1, 3):
-            along_a(d, e).wait_send()
+            if e > 0:
+                along_a(d, e).wait_send()
+            else:
+                own_along_a(d, 0).wait_send()
+                own_along_a(d, 1).wait_send()
         onward(e).wait_send()
         for d in range(4):
             across(d, e).wait_send()
@@ -401,7 +439,7 @@
             pltpu.VMEM((ROWS, LAT), f32),
             pltpu.VMEM((ROWS, 128), f32),
             pltpu.VMEM((CHUNK, 128), bf),
-            dma((9,)), dma((7,)), dma((7,)), dma((8,)), dma((8,)), dma((4,)), dma((4,)), dma((4, 4)), dma((4, 4)),
+            dma((9,)), dma((7,)), dma((7,)), dma((8,)), dma((8,)), dma((4, 2)), dma((4, 2)), dma((4, 5)), dma((4, 5)),
             dma((4, 4)), dma((4, 4)),
         ],
         name="cache_attention",

time: 50.3 us -> 48.9 us (0.972)
  Pallas kernels: 47.9 us -> 46.5 us
    pallas_call x1, Pallas kernels: 47.9 us -> 46.5 us  [body(): pl.pallas_call(kernel, out_shape=(pltpu.VMEM((rows, LAT), bf), pltpu.VMEM...]
where the time goes in v5:
time: 48.9 us; the launch traced here: 48.8 us
  Pallas kernels  46.5 us (95%)
  local copies, waits for them, and re-layouts  1.63 us (3%)
  between operations  0.64 us (1%)
    pallas_call x1, Pallas kernels, body(): pl.pallas_call(kernel, out_shape=(pltpu.VMEM((rows, LAT), bf), pltpu.VMEM...  46.5 us
    unnamed x2, local copies, waits for them, and re-layouts  1.63 us

profile of v5, /device:TPU:1, one launch (start us, length us, event | category | flops | bytes accessed | tf_op | source)
XLA Modules:
  0.0 48.8 jit_solution(5012733026857652407)
XLA Ops:
  0.6 46.5 %cache_attention.1 = (bf16[1024,512]{1,0:T(8,128)(2,1)S(1)}, bf16[32,2304]{1,0:T(8,128)(2,1)S(1)}) custom-call(bf16[128,896]{1,0:T(8,128)(2,1)} %hidden_hbm.1, bf16[576,896]{1,0:T(8,128)(2,1)} %bitcast.6, f32[1,512]{1,0:T(1,128)} %bitcast.7, f32[1,128]{1,0:T(1,128)} %constant.2.clone.freq_ref, bf16[8,576,128]{2,1,0:T(8,128)(2,1)} %bitcast.5, s32[64]{0:T(128)} %order_ref.1, ...), custom_call_target="tpu_custom_call" | custom-call | flops 8999999488 | bytes 4000000 | tf_op jit(solution)/shard_map/cache_attention/pallas_call | solution.py:414
  47.1 1.0 %copy.12 = bf16[128,8,512]{2,1,0:T(8,128)(2,1)} copy(bf16[128,8,512]{2,1,0:T(8,128)(2,1)S(1)} %bitcast.4) | data formatting | bytes 2097152
  48.1 0.7 %copy.13 = bf16[32,2304]{1,0:T(8,128)(2,1)} copy(bf16[32,2304]{1,0:T(8,128)(2,1)S(1)} %get-tuple-element.7) | data formatting | bytes 294912

commit v6 on v5

--- a/solution.py
+++ b/solution.py
@@ -256,7 +256,7 @@
                     zbuf[(z + STEPS[2 * pair]) % NZ, :, LAT:],
                     zbuf[(z + STEPS[2 * pair + 1]) % NZ, :, LAT:],
                 )
-        for e in (1, 3, 2):
+        for e in (1, 3):
             along_b(e, h).start()
         for d in (1, 3):
             own_along_a(d, h).start()
@@ -265,7 +265,9 @@
             for h in range(2):
                 came = some(block(0, e), h)
                 remote(came, came, b_send.at[e, h], b_recv.at[e, h], at_ab(a, (b + e) % 4)).wait_recv()
-            for d in (1, 3):
+                if (e, h) in ((1, 0), (3, 1)):
+                    remote(came, came, b_send.at[2, h], b_recv.at[2, h], at_ab(a, (b + e) % 4)).start()
+            for d in (1, 3) if e == 1 else (3, 1):
                 along_a(d, e).start()
         across(0, e).start()
         if e == 3:
@@ -347,7 +349,7 @@
 
         @pl.when(k == 0)
         def _():
-            for d, e in ((1, 1), (3, 1), (3, 3), (1, 3)):
+            for d, e in ((1, 1), (3, 3), (3, 1), (1, 3)):
                 take(d, e)
 
         @pl.when(k == 1)

time: 48.9 us -> 48.9 us (level)
  no operation moved by 1% of the time
where the time goes in v6:
time: 48.9 us; the launch traced here: 48.8 us
  Pallas kernels  46.5 us (95%)
  local copies, waits for them, and re-layouts  1.63 us (3%)
  between operations  0.64 us (1%)
    pallas_call x1, Pallas kernels, body(): pl.pallas_call(kernel, out_shape=(pltpu.VMEM((rows, LAT), bf), pltpu.VMEM...  46.5 us
    unnamed x2, local copies, waits for them, and re-layouts  1.63 us

profile of v6, /device:TPU:1, one launch (start us, length us, event | category | flops | bytes accessed | tf_op | source)
XLA Modules:
  0.0 48.8 jit_solution(4000802135250172367)
XLA Ops:
  0.6 46.5 %cache_attention.1 = (bf16[1024,512]{1,0:T(8,128)(2,1)S(1)}, bf16[32,2304]{1,0:T(8,128)(2,1)S(1)}) custom-call(bf16[128,896]{1,0:T(8,128)(2,1)} %hidden_hbm.1, bf16[576,896]{1,0:T(8,128)(2,1)} %bitcast.6, f32[1,512]{1,0:T(1,128)} %bitcast.7, f32[1,128]{1,0:T(1,128)} %constant.2.clone.freq_ref, bf16[8,576,128]{2,1,0:T(8,128)(2,1)} %bitcast.5, s32[64]{0:T(128)} %order_ref.1, ...), custom_call_target="tpu_custom_call" | custom-call | flops 8999999488 | bytes 4000000 | tf_op jit(solution)/shard_map/cache_attention/pallas_call | solution.py:416
  47.1 1.0 %copy.12 = bf16[128,8,512]{2,1,0:T(8,128)(2,1)} copy(bf16[128,8,512]{2,1,0:T(8,128)(2,1)S(1)} %bitcast.4) | data formatting | bytes 2097152
  48.1 0.7 %copy.13 = bf16[32,2304]{1,0:T(8,128)(2,1)} copy(bf16[32,2304]{1,0:T(8,128)(2,1)S(1)} %get-tuple-element.7) | data formatting | bytes 294912

commit v7 on v6

--- a/solution.py
+++ b/solution.py
@@ -337,6 +337,9 @@
         fold(high_rows, high, 4)
         fold(low_rows, low, 2)
 
+    for copy in scatter + along_z:
+        copy.wait_send()
+
     @pl.loop(0, 4)
     def _(k):
         @pl.when(k == 3)
@@ -373,8 +376,8 @@
 
     for k in range(4):
         low_span, high_span = slice(k * ROWS, (k + 1) * ROWS), slice((k + 4) * ROWS, (k + 5) * ROWS)
-        low = acc[low_span, :] / jnp.sum(den[low_span, :], axis=1, keepdims=True)
-        high = acc[high_span, :] / jnp.sum(den[high_span, :], axis=1, keepdims=True)
+        low = acc[low_span, :] * (1.0 / jnp.sum(den[low_span, :], axis=1, keepdims=True))
+        high = acc[high_span, :] * (1.0 / jnp.sum(den[high_span, :], axis=1, keepdims=True))
         swap = turn[:ROWS]
         out_ref[low_span, :] = jnp.where(swap, high, low).astype(jnp.bfloat16)
         out_ref[high_span, :] = jnp.where(swap, low, high).astype(jnp.bfloat16)
@@ -386,8 +389,6 @@
         paged_ref[:, j * width : j * width + LAT] = page_lat[span, :].astype(jnp.bfloat16)
         paged_ref[:, j * width + LAT : (j + 1) * width] = rotated[span, :].astype(jnp.bfloat16)
 
-    for copy in scatter + along_z:
-        copy.wait_send()
     for e in range(4):
         if e > 0:
             for h in range(2):

time: 48.9 us -> 48.9 us (level)
  no operation moved by 1% of the time
where the time goes in v7:
time: 48.9 us; the launch traced here: 48.7 us
  Pallas kernels  46.5 us (95%)
  local copies, waits for them, and re-layouts  1.63 us (3%)
  between operations  0.64 us (1%)
    pallas_call x1, Pallas kernels, body(): pl.pallas_call(kernel, out_shape=(pltpu.VMEM((rows, LAT), bf), pltpu.VMEM...  46.5 us
    unnamed x2, local copies, waits for them, and re-layouts  1.63 us

profile of v7, /device:TPU:1, one launch (start us, length us, event | category | flops | bytes accessed | tf_op | source)
XLA Modules:
  0.0 48.7 jit_solution(18076607975906978383)
XLA Ops:
  0.6 46.5 %cache_attention.1 = (bf16[1024,512]{1,0:T(8,128)(2,1)S(1)}, bf16[32,2304]{1,0:T(8,128)(2,1)S(1)}) custom-call(bf16[128,896]{1,0:T(8,128)(2,1)} %hidden_hbm.1, bf16[576,896]{1,0:T(8,128)(2,1)} %bitcast.6, f32[1,512]{1,0:T(1,128)} %bitcast.7, f32[1,128]{1,0:T(1,128)} %constant.2.clone.freq_ref, bf16[8,576,128]{2,1,0:T(8,128)(2,1)} %bitcast.5, s32[64]{0:T(128)} %order_ref.1, ...), custom_call_target="tpu_custom_call" | custom-call | flops 8999999488 | bytes 4000000 | tf_op jit(solution)/shard_map/cache_attention/pallas_call | solution.py:417
  47.1 1.0 %copy.12 = bf16[128,8,512]{2,1,0:T(8,128)(2,1)} copy(bf16[128,8,512]{2,1,0:T(8,128)(2,1)S(1)} %bitcast.4) | data formatting | bytes 2097152
  48.1 0.7 %copy.13 = bf16[32,2304]{1,0:T(8,128)(2,1)} copy(bf16[32,2304]{1,0:T(8,128)(2,1)S(1)} %get-tuple-element.7) | data formatting | bytes 294912
